TPU v7x, 256 devices: a whole 4x4x8 slice. The times are simulated.
256 devices in a mesh: field: 32 (over z, x_hi, core), row: 8 (over y, x_lo).
Axes of the slice: x: 4 (x_hi: 2, x_lo: 2; x = x_hi * 2 + x_lo), y: 4, z: 8, core: 2. Of those that a mesh axis runs over, the one named last changes fastest.
Arguments:
- direction: bfloat16 [32, 2, 512, 512], P('field', None, 'row'), may hold values from -6 to 6
- slits: int32 [64], P('field'), may hold values from 0 to 511
- sources: int32 [4], replicated, may hold values from 0 to 80
- support: int32 [512, 512], P('row'), may hold values from 0 to 1, as said below
- focus: float32 [3], replicated, may hold values from -2 to 2
- slit_focus: float32 [64], P('field'), may hold values from -1.5 to 1.5
- obj_rows: float32 [2, 576], replicated, may hold values from -6 to 6
- obj_cols: float32 [2, 576], replicated, may hold values from -6 to 6
- weights: float32 [4, 3, 128, 128], replicated, may hold values from 0.25 to 4
Outputs:
- curvature_product: float32 [32, 2, 512, 512], P('field', None, 'row')
Inputs may be any that keep to these rules, and one draw needn't show every extreme that they name: `support`: 1 where the pupil transmits, 0 elsewhere.
All inputs are finite; a program needn't handle non-finite values.
Results may differ from a plain program's by a relative error of at most 0.0022.
Values may be sent and summed in bfloat16 or wider, within the bound.
A program may use at most 192 MiB of HBM per device.

v0:
```python
import math

import jax
import jax.numpy as jnp
from jax import lax
from jax.sharding import PartitionSpec as P

N = 512
K = 8
J = 4
M = 128
SLIT_GRID = 512
SRC_SIDE = 9
SHIFT = 8
PAD = 32


def legendre(slits):
    position = (2.0 * slits.astype(jnp.float32) + 1.0) / SLIT_GRID - 1.0
    values = [jnp.ones_like(position), position]
    for order in range(1, K - 1):
        values.append(
            ((2.0 * order + 1.0) * position * values[order] - order * values[order - 1])
            / (order + 1.0)
        )
    return jnp.stack(values[:K], axis=1)


def tables(sources, defocus, obj_rows, obj_cols):
    freq = jnp.arange(N, dtype=jnp.int32)
    radial = ((2 * freq - N + 1).astype(jnp.float32) / N) ** 2
    theta = math.pi * defocus[:, :, None] * radial[None, None, :]
    turn_cos = jnp.cos(theta)
    turn_sin = jnp.sin(theta)
    middle = SRC_SIDE // 2
    row_shift = SHIFT * (sources // SRC_SIDE - middle)
    col_shift = SHIFT * (sources % SRC_SIDE - middle)

    def window(spectrum, offset):
        return lax.dynamic_slice_in_dim(spectrum, PAD - offset, N, 1)

    def factor(spectrum, offsets):
        picked = jax.vmap(window, in_axes=(None, 0))(spectrum, offsets)
        first = picked[None, :, None, 0, :]
        second = picked[None, :, None, 1, :]
        real_part = first * turn_cos[:, None] - second * turn_sin[:, None]
        imag_part = first * turn_sin[:, None] + second * turn_cos[:, None]
        return (real_part, imag_part)

    def kernel(stretch):
        centered = (freq - N // 2)[:, None] * (jnp.arange(M, dtype=jnp.int32) - M // 2)[None, :]
        angle = jnp.mod(stretch * centered, N).astype(jnp.float32) * (-2.0 * math.pi / N)
        scale = 1.0 / math.sqrt(M)
        return (jnp.cos(angle) * scale, jnp.sin(angle) * scale)

    def apply(fac_re, fac_im, ker_re, ker_im):
        real_part = fac_re[..., None] * ker_re - fac_im[..., None] * ker_im
        imag_part = fac_re[..., None] * ker_im + fac_im[..., None] * ker_re
        return (real_part.astype(jnp.bfloat16), imag_part.astype(jnp.bfloat16))

    col_re, col_im = factor(obj_cols, col_shift)
    ker_re, ker_im = kernel(1)
    map_re, map_im = apply(col_re, col_im, ker_re, ker_im)
    upper = jnp.stack([map_re, map_im], axis=4)
    lower = jnp.stack([-map_im, map_re], axis=4)
    block = jnp.stack([upper, lower], axis=3)
    block = block.reshape(block.shape[0], block.shape[1], block.shape[2], 2 * N, 2 * M)
    row_re, row_im = factor(obj_rows, row_shift)
    ker_re, ker_im = kernel(2)
    rows_re, rows_im = apply(row_re, row_im, ker_re, ker_im)
    return (block, rows_re, rows_im)


def selector(basis_part, count):
    term_index = jnp.arange(count, dtype=jnp.int32)
    term_pick = ((term_index // J)[None, :] == jnp.arange(K, dtype=jnp.int32)[:, None]).astype(
        jnp.bfloat16
    )
    jones_pick = ((term_index % J)[None, :] == jnp.arange(J, dtype=jnp.int32)[:, None]).astype(
        jnp.float32
    )
    picked = jnp.dot(basis_part, term_pick, preferred_element_type=jnp.float32)
    return (picked[:, None, :] * jones_pick[None]).astype(jnp.bfloat16)


def forward_rows(row_re, row_im, spectra):
    primary = jnp.einsum("izno,izny->izoy", row_re, spectra, preferred_element_type=jnp.float32)
    second = jnp.einsum("izno,izny->izoy", row_im, spectra, preferred_element_type=jnp.float32)
    shape = primary.shape[:3] + (2, primary.shape[3] // 2)
    primary = primary.reshape(shape)
    second = second.reshape(shape)
    image = jnp.stack(
        [primary[..., 0, :] - second[..., 1, :], primary[..., 1, :] + second[..., 0, :]], axis=3
    )
    return image.reshape(shape[:3] + (2 * shape[4],))


def backward_rows(row_re, row_im, scaled):
    back_one = jnp.einsum("izno,izoy->izny", row_re, scaled, preferred_element_type=jnp.float32)
    back_two = jnp.einsum("izno,izoy->izny", row_im, scaled, preferred_element_type=jnp.float32)
    shape = back_one.shape[:3] + (2, back_one.shape[3] // 2)
    back_one = back_one.reshape(shape)
    back_two = back_two.reshape(shape)
    adjoint = jnp.stack(
        [back_one[..., 0, :] + back_two[..., 1, :], back_one[..., 1, :] - back_two[..., 0, :]],
        axis=3,
    )
    return adjoint.reshape(shape[:3] + (2 * shape[4],)).astype(jnp.bfloat16)


def weighted_adjoint(image, weights, source, table_row, rows_re, rows_im, plane_count):
    count = image.shape[0]
    picked_weights = jnp.take(weights, source, axis=0)
    scaled = image.reshape(count, plane_count, M, 2, M) * picked_weights[:, :, :, None, :]
    scaled = scaled.astype(jnp.bfloat16).reshape(count, plane_count, M, 2 * M)
    return backward_rows(
        jnp.take(rows_re, table_row, axis=0), jnp.take(rows_im, table_row, axis=0), scaled
    )


def local(direction, slits, sources, support, focus, slit_focus, obj_rows, obj_cols, weights):
    row_count = lax.axis_size("row")
    field_count = lax.axis_size("field")
    local_rows = direction.shape[2]
    own_terms = direction.shape[0]
    slit_count = slits.shape[0]
    src_count = sources.shape[0]
    plane_count = focus.shape[0]
    defocus = focus[None, :] + slit_focus[:, None]
    basis = legendre(slits).astype(jnp.bfloat16)
    mask = support.astype(jnp.float32)
    coeff_piece = lax.all_gather(direction, "field", axis=0, tiled=True)
    chosen = selector(basis, coeff_piece.shape[0])
    summed = jnp.einsum("sjt,tcrn->sjrcn", chosen, coeff_piece, preferred_element_type=jnp.float32)
    pupil = (summed * mask[None, None, :, None, :]).astype(jnp.bfloat16)
    pupil = pupil.reshape(slit_count * J, local_rows, 2 * N)
    block, rows_re, rows_im = tables(sources, defocus, obj_rows, obj_cols)
    rows_re = rows_re.reshape(slit_count * src_count, plane_count, N, M)
    rows_im = rows_im.reshape(slit_count * src_count, plane_count, N, M)
    pupil_four = pupil.reshape(slit_count, J, local_rows, 2 * N)
    item_count = slit_count * J * src_count
    own_items = item_count // row_count
    item_start = lax.axis_index("row") * own_items
    own_order = item_start + jnp.arange(own_items, dtype=jnp.int32)
    own_source = own_order % src_count
    own_table = own_order // (J * src_count) * src_count + own_source
    spectra = jnp.einsum(
        "sjrc,sqzcy->sjqzry", pupil_four, block, preferred_element_type=jnp.float32
    ).astype(jnp.bfloat16)
    spectra = spectra.reshape(item_count, plane_count, local_rows, 2 * M)
    moved = lax.all_to_all(spectra, "row", split_axis=0, concat_axis=2, tiled=True)
    image = forward_rows(
        jnp.take(rows_re, own_table, axis=0), jnp.take(rows_im, own_table, axis=0), moved
    )
    adjoint = weighted_adjoint(image, weights, own_source, own_table, rows_re, rows_im, plane_count)
    returned = lax.all_to_all(adjoint, "row", split_axis=2, concat_axis=0, tiled=True)
    returned = returned.reshape(slit_count, J, src_count, plane_count, local_rows, 2 * M)
    pulled = jnp.einsum("sjqzry,sqzcy->sjrc", returned, block, preferred_element_type=jnp.float32)
    pulled = pulled.reshape(slit_count, J, local_rows, 2, N) * mask[None, None, :, None, :]
    pulled = pulled.astype(jnp.bfloat16)
    chosen = selector(basis, own_terms * lax.axis_size("field"))
    gathered = lax.psum_scatter(
        jnp.einsum("sjt,sjrcn->tcrn", chosen, pulled, preferred_element_type=jnp.float32),
        "field",
        scatter_dimension=0,
        tiled=True,
    )
    factor = 4.0 / (src_count * plane_count * slit_count * field_count)
    return gathered * factor


def solution(mesh):
    return jax.shard_map(
        local,
        mesh=mesh,
        in_specs=(
            P("field", None, "row", None),
            P("field"),
            P(),
            P("row", None),
            P(),
            P("field"),
            P(),
            P(),
            P(),
        ),
        out_specs=P("field", None, "row", None),
        check_vma=False,
    )
```

profile of v0, /device:TPU:6, one launch (start us, length us, event | category | flops | bytes accessed | tf_op | source)
XLA Modules:
  0.0 473.5 jit_solution(13888669130428593978)
XLA Ops:
  6.5 0.7 all-gather.2.cloned.1.call-update
  7.3 1.2 fusion.54
  8.5 8.1 %while.3 = (s32[]{:T(128)}, f32[2,576]{1,0:T(2,128)}, s32[4,2]{0,1:T(2,128)S(1)}, f32[4,2,512]{2,1,0:T(2,128)S(1)}, s32[]{:T(128)}) while((s32[]{:T(128)}, f32[2,576]{1,0:T(2,128)}, s32[4,2]{0,1:T(2,128)S(1)}, f32[4,2,512]{2,1,0:T(2,128)S(1)}, s32[]{:T(128)}) %tuple.55), condition=%wide.while_cond.1, body=%wide.while_body.1.sunk | while | flops 2 | bytes 8289 | solution.py:40
  8.6 0.5 slice.103
  9.2 1.4 bitcast_dynamic-update-slice_fusion.5
  10.6 0.5 slice.103
  11.2 1.4 bitcast_dynamic-update-slice_fusion.5
  12.6 0.5 slice.103
  13.2 1.4 bitcast_dynamic-update-slice_fusion.5
  14.7 0.5 slice.103
  15.2 1.4 bitcast_dynamic-update-slice_fusion.5
  16.6 0.7 add_multiply_fusion
  17.6 2.1 cosine_multiply_fusion.1
  19.8 28.5 %fusion.61 = (bf16[2,4,3,512,1,128]{5,4,3,2,1,0:T(2,128)(2,1)S(1)}, bf16[2,4,3,512,1,128]{5,4,3,2,1,0:T(2,128)(2,1)S(1)}) fusion(f32[512,128]{1,0:T(8,128)S(1)} %get-tuple-element.68, f32[2,4,3,512]{3,2,1,0:T(4,128)S(1)} %get-tuple-element.58, f32[512,128]{1,0:T(8,128)S(1)} %get-tuple-element.67, f32[2,4,3,512]{3,2,1,0:T(4,128)S(1)} %get-tuple-element.57), kind=kLoop, calls=%fused_computation.146 | loop fusion | flops 7864320 | bytes 6914048 | tf_op jit(solution)/shard_map/neg | solution.py:65
  48.3 28.5 %subtract_convert_fusion = bf16[2,4,3,512,1,128]{5,4,3,2,1,0:T(2,128)(2,1)S(1)} fusion(f32[512,128]{1,0:T(8,128)S(1)} %get-tuple-element.67, f32[2,4,3,512]{3,2,1,0:T(4,128)S(1)} %get-tuple-element.58, f32[512,128]{1,0:T(8,128)S(1)} %get-tuple-element.68, f32[2,4,3,512]{3,2,1,0:T(4,128)S(1)} %get-tuple-element.57), kind=kLoop, calls=%fused_computation.16 | loop fusion | flops 6291456 | bytes 3768320 | tf_op jit(solution)/shard_map/convert_element_type | solution.py:59
  76.8 29.6 %maximum_bitcast_fusion = (bf16[2,4,3,1,512,2,128]{6,5,4,3,2,1,0:T(2,128)(2,1)S(1)}, bf16[2,4,3,1,512,2,128]{6,5,4,3,2,1,0:T(2,128)(2,1)}) fusion(bf16[2,4,3,512,1,128]{5,4,3,2,1,0:T(2,128)(2,1)S(1)} %get-tuple-element.44, bf16[2,4,3,512,1,128]{5,4,3,2,1,0:T(2,128)(2,1)S(1)} %subtract_convert_fusion, bf16[2,4,3,512,1,128]{5,4,3,2,1,0:T(2,128)(2,1)S(1)} %get-tuple-element.43), kind=kLoop, calls=%fused_computation.12 | loop fusion | flops 25165824 | bytes 22020096 | tf_op jit(solution)/shard_map/stack | solution.py:66
  106.4 21.0 %pad_maximum_fusion = bf16[2,4,3,2,512,2,128]{6,5,4,3,2,1,0:T(2,128)(2,1)} fusion(bf16[2,4,3,1,512,2,128]{6,5,4,3,2,1,0:T(2,128)(2,1)} %get-tuple-element.48, bf16[2,4,3,1,512,2,128]{6,5,4,3,2,1,0:T(2,128)(2,1)S(1)} %get-tuple-element.47), kind=kLoop, calls=%fused_computation.7 | loop fusion | flops 6291456 | bytes 25165824 | tf_op jit(solution)/shard_map/stack | solution.py:66
  127.4 20.5 %reshape.466 = bf16[2,4,3,1024,256,1]{4,3,2,1,0,5:T(8,128)(2,1)} reshape(bf16[2,4,3,2,512,2,128]{6,5,4,3,2,1,0:T(2,128)(2,1)} %pad_maximum_fusion) | data formatting | bytes 25165824 | tf_op jit(solution)/shard_map/reshape | solution.py:67
  149.0 0.5 copy-done.9
  149.6 4.8 %fusion.18 = bf16[2,4,64,2,512]{4,1,2,3,0:T(4,128)(2,1)S(1)} fusion(bf16[32,2,64,512]{3,2,1,0:T(8,128)(2,1)} %all-gather.2.cloned.1.call-done, f32[64,512]{1,0:T(8,128)S(1)} %convert_element_type.127, f32[4,32]{1,0:T(4,128)S(1)} %fusion.49, f32[2,32]{1,0:T(2,128)S(1)} %fusion.39), kind=kOutput, calls=%fused_computation.36 | convolution fusion | flops 34603520 | bytes 5374720 | tf_op jit(solution)/shard_map/sjt,tcrn->sjrcn/dot_general | solution.py:134
  154.4 1.1 copy.117
  155.5 0.9 reshape.467
  156.5 9.3 %convert_bitcast_fusion = bf16[2,4,4,3,64,256]{5,4,1,3,2,0:T(8,128)(2,1)} fusion(bf16[2,4,3,1024,256,1]{4,3,2,1,0,5:T(8,128)(2,1)} %reshape.466, bf16[2,4,64,1024,1,1]{3,2,1,0,4,5:T(8,128)(2,1)S(1)} %reshape.467), kind=kOutput, calls=%fused_computation.27 | convolution fusion | flops 3222798336 | bytes 16777216 | tf_op jit(solution)/shard_map/sjrc,sqzcy->sjqzry/dot_general | solution.py:147
  165.8 3.9 copy.118
  169.7 6.1 %all-to-all-start = ((bf16[32,3,64,256]{3,2,1,0:T(8,128)(2,1)}), bf16[32,3,64,256]{3,2,1,0:T(8,128)(2,1)}, u32[]{:S(2)}, u32[]{:S(2)}) async-start(bf16[32,3,64,256]{3,2,1,0:T(8,128)(2,1)} %bitcast.131), calls=%async_computation | async-start | bytes 6291456 | tf_op jit(solution)/shard_map/all_to_all | solution.py:151
  175.8 4.8 %while.2 = (s32[]{:T(128)}, f32[2,576]{1,0:T(2,128)S(1)}, s32[4,2]{0,1:T(2,128)S(1)}, f32[4,2,512]{2,1,0:T(2,128)S(1)}, s32[]{:T(128)}) while((s32[]{:T(128)}, f32[2,576]{1,0:T(2,128)S(1)}, s32[4,2]{0,1:T(2,128)S(1)}, f32[4,2,512]{2,1,0:T(2,128)S(1)}, s32[]{:T(128)}) %tuple.65), condition=%wide.while_cond, body=%wide.while_body.sunk | while | flops 2 | bytes 8289 | solution.py:40
  175.9 0.5 slice.102
  176.4 0.6 bitcast_dynamic-update-slice_fusion.4
  177.1 0.5 slice.102
  177.6 0.6 bitcast_dynamic-update-slice_fusion.4
  178.3 0.5 slice.102
  178.8 0.6 bitcast_dynamic-update-slice_fusion.4
  179.5 0.5 slice.102
  180.0 0.6 bitcast_dynamic-update-slice_fusion.4
  180.8 6.1 %add_convert_fusion = (bf16[8,3,512,128]{3,2,1,0:T(8,128)(2,1)}, bf16[8,3,512,128]{3,2,1,0:T(8,128)(2,1)}) fusion(f32[512,128]{1,0:T(8,128)S(1)} %get-tuple-element.66, f32[8,3,512]{2,1,0:T(4,128)S(1)} %get-tuple-element.56, f32[512,128]{1,0:T(8,128)S(1)} %get-tuple-element.65, f32[8,3,512]{2,1,0:T(4,128)S(1)} %get-tuple-element.55), kind=kLoop, calls=%fused_computation.14 | loop fusion | flops 12582912 | bytes 6914048 | tf_op jit(solution)/shard_map/convert_element_type | solution.py:59
  186.9 2.7 gather_fusion.2
  189.6 3.8 gather_fusion.1
  193.5 0.6 gather_fusion
  194.3 18.7 %all-to-all-done = bf16[32,3,64,256]{3,2,1,0:T(8,128)(2,1)} async-done(((bf16[32,3,64,256]{3,2,1,0:T(8,128)(2,1)}), bf16[32,3,64,256]{3,2,1,0:T(8,128)(2,1)}, u32[]{:S(2)}, u32[]{:S(2)}) %all-to-all-start) | async-done | bytes 3145760 | tf_op jit(solution)/shard_map/all_to_all | solution.py:151
  212.9 2.3 copy.119
  215.2 1.1 fusion.27
  216.4 0.5 copy-done.2
  216.8 1.2 fusion.62
  218.1 1.4 copy.150
  219.5 3.5 fusion.25
  223.0 1.3 fusion.63
  224.3 2.3 copy.149
  226.6 2.3 copy.152
  228.8 2.3 copy.151
  231.1 1.2 sub.142
  232.3 1.5 add.241
  234.4 2.5 fusion.24
  236.8 1.0 fusion.26
  237.9 1.9 fusion.8
  239.8 1.9 pad_maximum_fusion.1
  241.7 6.1 %copy.129 = bf16[4,3,512,256]{3,0,1,2:T(4,128)(2,1)} copy(bf16[4,3,512,256]{2,3,1,0:T(8,128)(2,1)} %bitcast.132) | data formatting | bytes 6291456 | tf_op jit(solution)/shard_map/convert_element_type | solution.py:108
  247.8 41.1 %all_to_all.33 = bf16[4,3,512,256]{3,0,1,2:T(4,128)(2,1)S(1)} all-to-all(bf16[4,3,512,256]{3,0,1,2:T(4,128)(2,1)} %copy.129), channel_id=1, replica_groups=mesh['field'=32,'row'=8] {'row'}, dimensions={2} | all-to-all | bytes 6291456 | tf_op jit(solution)/shard_map/all_to_all | solution.py:156
  288.9 0.5 copy.130
  289.7 7.8 %fusion.12 = f32[2,4,64,1024]{3,2,1,0:T(8,128)} fusion(bf16[2,4,4,3,64,256]{5,4,3,2,1,0:T(8,128)(2,1)S(1)} %bitcast.138, bf16[2,4,3,1024,256,1]{4,3,2,1,0,5:T(8,128)(2,1)} %reshape.466), kind=kOutput, calls=%fused_computation.31 | convolution fusion | flops 3221225472 | bytes 17825792 | tf_op jit(solution)/shard_map/sjqzry,sqzcy->sjrc/dot_general | solution.py:158
  297.6 3.0 reshape.395
  300.6 2.2 convolution_bitcast_fusion
  302.8 8.1 %copy.133 = f32[32,2,64,512]{3,2,1,0:T(8,128)} copy(f32[32,2,64,512]{3,0,1,2:T(8,128)S(1)} %convolution_bitcast_fusion) | data formatting | bytes 16777216 | tf_op jit(solution)/shard_map/sjt,sjrcn->tcrn/transpose | solution.py:163
  311.0 154.0 %reduce-scatter.2.cloned.1.call-done = f32[1,2,64,512]{3,2,1,0:T(8,128)} async-done(((f32[32,2,64,512]{3,2,1,0:T(8,128)}), f32[1,2,64,512]{3,2,1,0:T(8,128)}) %reduce-scatter.2.cloned.1.call-update) | async-done | bytes 262160 | tf_op jit(solution)/shard_map/reduce_scatter | solution.py:162
  465.0 1.7 broadcast_multiply_fusion
  (80 shorter events, 3.2 us)
Async XLA Ops:
  6.5 186.9 %copy-start = (f32[4,3,128,128]{3,2,1,0:T(8,128)S(1)}, f32[4,3,128,128]{3,2,1,0:T(8,128)}, u32[]{:S(2)}) copy-start(f32[4,3,128,128]{3,2,1,0:T(8,128)} %param.19) | copy-start | bytes 2359300
  6.5 142.5 %all-gather.2.cloned.1.call-start = ((), (), s32[]{:S(2)}) async-start(), calls=%async_computation.3 | async-start | bytes 4325376 | tf_op jit(solution)/shard_map/all_gather | solution.py:132
  17.6 30.7 %copy-start.3 = (f32[2,3,512]{2,1,0:T(4,128)}, f32[2,3,512]{2,1,0:T(4,128)S(1)}, u32[]{:S(2)}) copy-start(f32[2,3,512]{2,1,0:T(4,128)S(1)} %get-tuple-element.64) | copy-start | bytes 36868
  127.4 20.6 %copy-start.12 = (s32[2]{0:T(128)S(1)}, s32[2]{0:T(128)}, u32[]{:S(2)}) copy-start(s32[2]{0:T(128)} %param.12) | copy-start | bytes 28
  127.4 21.4 %copy-start.5 = (s32[64,512]{1,0:T(8,128)S(1)}, s32[64,512]{1,0:T(8,128)}, u32[]{:S(2)}) copy-start(s32[64,512]{1,0:T(8,128)} %param.14) | copy-start | bytes 393220
  149.0 0.6 copy-start.9
  149.0 0.6 copy-start.7
  169.7 6.1 %copy-start.11 = (s32[4,1]{0,1:T(1,128)S(1)}, s32[4,1]{0,1:T(1,128)}, u32[]{:S(2)}) copy-start(s32[4,1]{0,1:T(1,128)} %get-tuple-element.69) | copy-start | bytes 52
  169.7 6.1 %copy-start.6 = (f32[2,576]{1,0:T(2,128)S(1)}, f32[2,576]{1,0:T(2,128)}, u32[]{:S(2)}) copy-start(f32[2,576]{1,0:T(2,128)} %param.17) | copy-start | bytes 13828
  169.7 11.0 %copy-start.4 = (f32[2,3,512]{2,1,0:T(4,128)S(1)}, f32[2,3,512]{2,1,0:T(4,128)}, u32[]{:S(2)}) copy-start(f32[2,3,512]{2,1,0:T(4,128)} %copy-done.3) | copy-start | bytes 36868
  169.7 43.2 %all-to-all-start = ((bf16[32,3,64,256]{3,2,1,0:T(8,128)(2,1)}), bf16[32,3,64,256]{3,2,1,0:T(8,128)(2,1)}, u32[]{:S(2)}, u32[]{:S(2)}) async-start(bf16[32,3,64,256]{3,2,1,0:T(8,128)(2,1)} %bitcast.131), calls=%async_computation | async-start | bytes 6291456 | tf_op jit(solution)/shard_map/all_to_all | solution.py:151
  175.8 289.2 %reduce-scatter.2.cloned.1.call-start = ((), (), s32[]{:S(2)}) async-start(), calls=%async_computation.4 | async-start | bytes 8650752 | tf_op jit(solution)/shard_map/reduce_scatter | solution.py:162
  215.2 1.6 copy-start.2
  297.6 3.0 copy-start.8
  297.6 3.1 copy-start.10
  311.0 155.7 %copy-start.1 = (f32[4,3,128,128]{3,2,1,0:T(8,128)S(1)}, f32[4,3,128,128]{3,2,1,0:T(8,128)}, u32[]{:S(2)}) copy-start(f32[4,3,128,128]{3,2,1,0:T(8,128)} %param.19) | copy-start | bytes 2359300
Sparse Core Ops, SparseCore 0:
  10.1 88.1 all-gather.1
  311.1 153.8 reduce-scatter.1
where the time goes:
time: 477 us; the launch traced here: 473 us
  waiting for transfers between devices  173 us (36%)
  other arithmetic  127 us (27%)
  local copies, waits for them, and re-layouts  80 us (17%)
  blocking collectives  41.1 us (9%)
  matrix products  32.4 us (7%)
  between operations  13.8 us (3%)
  starting transfers between devices  6.06 us (1%)
    reduce_scatter x1, waiting for transfers between devices, local(): lax.psum_scatter(jnp.einsum('sjt,sjrcn->tcrn', chosen, pulled, preferred_...  154 us
    another operation x2, other arithmetic, tables(): block = jnp.stack([upper, lower], axis=3)  50.6 us
    all_to_all x1, blocking collectives, local(): lax.all_to_all(adjoint, 'row', split_axis=2, concat_axis=0, tiled=True)  41.1 us
    convert_element_type x2, other arithmetic, apply(): return (real_part.astype(jnp.bfloat16), imag_part.astype(jnp.bfloat16))  34.6 us
    neg x1, other arithmetic, tables(): lower = jnp.stack([-map_im, map_re], axis=4)  28.5 us
    reshape x1, local copies, waits for them, and re-layouts, tables(): block.reshape(block.shape[0], block.shape[1], block.shape[2], 2 * N, 2 * M)  20.5 us
    all_to_all x1, waiting for transfers between devices, local(): lax.all_to_all(spectra, 'row', split_axis=0, concat_axis=2, tiled=True)  18.7 us
    gather x24, local copies, waits for them, and re-layouts  12.8 us
  transfers between devices with their start and end apart: 3, of which 2 were waited for; matrix products, arithmetic and copies ran while one was open for 34% of the time, Pallas kernels for 0%

commit v1 on v0

v1 whole, which is shorter than its diff:
```python
import functools
import math

import jax
import jax.numpy as jnp
import numpy as np
from jax import lax
from jax.experimental import pallas as pl
from jax.experimental.pallas import tpu as pltpu
from jax.sharding import PartitionSpec as P

J = 4
M = 128
SLIT_GRID = 512
SRC_SIDE = 9
SHIFT = 8
PAD = 32
GROUPS = 4
MESH = pl.DeviceIdType.MESH
NT = (((1,), (1,)), ((), ()))


def kernel_tables(size, blocks, groups):
    freq = np.arange(size)
    span = size // (blocks * groups)
    order = freq.reshape(blocks, groups, span).transpose(1, 0, 2).reshape(-1)

    def kernel(stretch):
        turns = np.mod(stretch * (freq - size // 2)[:, None] * (np.arange(M) - M // 2)[None, :], size)
        angle = (turns.astype(np.float32) * np.float32(-2.0 * math.pi / size)).astype(np.float64)
        scale = 1.0 / math.sqrt(M)
        return np.stack([np.cos(angle) * scale, np.sin(angle) * scale]).astype(np.float32)

    cols = np.ascontiguousarray(kernel(1).transpose(0, 2, 1))
    rows = np.ascontiguousarray(kernel(2)[:, order])
    return cols, np.ascontiguousarray(rows.transpose(0, 2, 1)), rows


def body(sizes, slits, sources, focus, slit_focus, direction, support, obj_rows, obj_cols, weights,
         cols_t_hbm, rows_t_hbm, rows_hbm, out,
         cols_t, rows_t, rows, wts, info, coeff, mix, mix_t, fac, fac_t, fac_p, block_t, row_t, row_n,
         pupil_out, pupil_in, image, adjoint, pulled, returned, part, partial_in,
         load_sem, info_send, info_recv, ag_send, ag_recv, out_send, out_recv, back_send, back_recv, rs_send, rs_recv):
    ring, row_count, src_count, plane_count, size, total_slits = sizes
    groups = GROUPS
    span = size // (row_count * groups)
    slab = span * row_count
    bands = src_count * plane_count
    half = ring // 2
    me_f, me_r = lax.axis_index("field"), lax.axis_index("row")
    z, j = me_f // J, me_f % J
    y, x = me_r // 2, me_r % 2
    y_count = row_count // 2
    right = (((z + 1) % ring) * J + j, me_r)
    left = (((z + ring - 1) % ring) * J + j, me_r)
    siblings = [(z * J + (j + d) % J, me_r) for d in range(1, J)]
    steps = [(dy, dx) for dy in (2, 1, 3, 0) for dx in (1, 0) if dy < y_count and (dy, dx) != (0, 0)]
    peers = [((y + dy) % y_count) * 2 + (x + dx) % 2 for dy, dx in steps]

    loads = [
        pltpu.make_async_copy(src, dst, load_sem.at[i])
        for i, (src, dst) in enumerate(
            [(cols_t_hbm, cols_t), (rows_t_hbm, rows_t), (rows_hbm, rows), (weights, wts)]
        )
    ]
    for load in loads:
        load.start()

    barrier = pltpu.get_barrier_semaphore()
    greeted = [right, left] + siblings + [(me_f, peer) for peer in peers]
    for device in greeted:
        pl.semaphore_signal(barrier, inc=1, device_id=device, device_id_type=MESH)

    for g in range(groups):
        mask = support[g * span : (g + 1) * span, :].astype(jnp.float32)
        for c in range(2):
            own = direction[0, c, g * span : (g + 1) * span, :].astype(jnp.float32) * mask
            coeff[g, pl.ds(z * span, span), c * size : (c + 1) * size] = own.astype(jnp.bfloat16)
    for i in range(2):
        position = (2.0 * slits[i].astype(jnp.float32) + 1.0) / SLIT_GRID - 1.0
        info[j, i * span : (i + 1) * span, :] = jnp.full((span, 128), position, jnp.float32)
        info[j, (2 + i) * span : (3 + i) * span, :] = jnp.full((span, 128), slit_focus[i], jnp.float32)

    pl.semaphore_wait(barrier, len(greeted))

    sent = []

    def send(src, dst, send_sem, recv_sem, device):
        copy = pltpu.make_async_remote_copy(
            src_ref=src, dst_ref=dst, send_sem=send_sem, recv_sem=recv_sem, device_id=device, device_id_type=MESH
        )
        copy.start()
        sent.append(copy)

    def arrived(dst, send_sem, recv_sem, device):
        pltpu.make_async_remote_copy(
            src_ref=dst, dst_ref=dst, send_sem=send_sem, recv_sem=recv_sem, device_id=device, device_id_type=MESH
        ).wait_recv()

    def hops(way, g):
        return half if way == g % 2 else half - 1

    def ring_to(way):
        return right if way == 0 else left

    def gather_slot(way, g, h):
        k = (z + ring - h) % ring if way == 0 else (z + h) % ring
        return coeff.at[g, pl.ds(pl.multiple_of(k * span, span), span), :]

    def gather_send(way, g, h):
        slot = gather_slot(way, g, h)
        send(slot, slot, ag_send.at[way, g, h], ag_recv.at[way, g, h], ring_to(way))

    def gather_arrived(way, g, h):
        arrived(gather_slot(way, g, h + 1), ag_send.at[way, g, h], ag_recv.at[way, g, h], ring_to(way))

    for d, device in enumerate(siblings):
        send(info.at[j], info.at[j], info_send.at[d], info_recv.at[d], device)
    for g in range(groups):
        for way in range(2):
            gather_send(way, g, 0)

    for d, device in enumerate(siblings):
        source = (j + J - 1 - d) % J
        arrived(info.at[source], info_send.at[d], info_recv.at[d], device)
    own_focus = info[me_r // 2, pl.ds((2 + me_r % 2) * span, 8), :]
    own_focus = jnp.concatenate([own_focus] * (size // 128), axis=1)
    which = lax.broadcasted_iota(jnp.int32, (8, size), 0)
    plane = jnp.full((8, size), focus[0], jnp.float32)
    for p in range(1, plane_count):
        plane = jnp.where(which == p, focus[p], plane)
    freq = lax.broadcasted_iota(jnp.int32, (8, size), 1)
    scaled = (2 * freq - size + 1).astype(jnp.float32) / size
    theta = math.pi * (plane + own_focus) * (scaled * scaled)
    turn_cos, turn_sin = jnp.cos(theta), jnp.sin(theta)
    middle = SRC_SIDE // 2
    for q in range(src_count):
        for base, spectrum, place in ((0, obj_rows, sources[q] // SRC_SIDE), (64, obj_cols, sources[q] % SRC_SIDE)):
            picked = spectrum[:, PAD + SHIFT * middle : PAD + SHIFT * middle + size]
            for v in range(1, SRC_SIDE):
                start = PAD - SHIFT * (v - middle)
                picked = jnp.where(place == v, spectrum[:, start : start + size], picked)
            first, second = picked[0:1], picked[1:2]
            fac[base + 8 * q : base + 8 * q + 8, :] = first * turn_cos - second * turn_sin
            fac[base + 32 + 8 * q : base + 40 + 8 * q, :] = first * turn_sin + second * turn_cos
    turned = fac[...].T
    for g in range(groups):
        for r in range(row_count):
            start = r * groups * span + g * span
            fac_t[g * slab + r * span : g * slab + (r + 1) * span, :] = turned[start : start + span, :]
    fac_p[...] = fac_t[...].T

    edge = row_count * span
    position = jnp.concatenate([info[s, 0 : 2 * span, :] for s in range(J)], axis=0)
    position = jnp.concatenate([position] * (edge // 128), axis=1) if edge > 128 else position
    sub = lax.broadcasted_iota(jnp.int32, (edge, edge), 0)
    lane = lax.broadcasted_iota(jnp.int32, (edge, edge), 1)
    before, now = jnp.ones_like(position), position
    chosen = jnp.where(lane // span == 0, before, jnp.where(lane // span == 1, now, 0.0))
    for order in range(1, ring - 1):
        before, now = now, ((2.0 * order + 1.0) * position * now - order * before) / (order + 1.0)
        chosen = jnp.where(lane // span == order + 1, now, chosen)
    chosen = jnp.where(sub % span == lane % span, chosen, 0.0)
    mix[...] = chosen.astype(jnp.bfloat16)
    mix_t[...] = chosen.T.astype(jnp.bfloat16)

    for load in loads:
        load.wait()

    def build_lanes(band, carry):
        index = (band // plane_count) * 8 + band % plane_count
        cf_re, cf_im = fac[pl.ds(64 + index, 1), :], fac[pl.ds(96 + index, 1), :]
        rf_re, rf_im = fac_p[pl.ds(index, 1), :], fac_p[pl.ds(32 + index, 1), :]
        base = pl.multiple_of(band * 2 * M, 2 * M)
        for m in range(0, M, 16):
            ker_re, ker_im = cols_t[0, m : m + 16, :], cols_t[1, m : m + 16, :]
            real = (cf_re * ker_re - cf_im * ker_im).astype(jnp.bfloat16)
            imag = (cf_re * ker_im + cf_im * ker_re).astype(jnp.bfloat16)
            block_t[pl.ds(base + m, 16), 0:size] = real
            block_t[pl.ds(base + m, 16), size : 2 * size] = -imag
            block_t[pl.ds(base + M + m, 16), 0:size] = imag
            block_t[pl.ds(base + M + m, 16), size : 2 * size] = real
            ker_re, ker_im = rows_t[0, m : m + 16, :], rows_t[1, m : m + 16, :]
            row_t[pl.ds(base + m, 16), :] = (rf_re * ker_re - rf_im * ker_im).astype(jnp.bfloat16)
            row_t[pl.ds(base + M + m, 16), :] = (rf_re * ker_im + rf_im * ker_re).astype(jnp.bfloat16)
        return carry

    def build_sublanes(step, carry):
        start = pl.multiple_of(step * 32, 32)
        ker_re, ker_im = rows[0, pl.ds(start, 32), :], rows[1, pl.ds(start, 32), :]
        held = fac_t[pl.ds(start, 32), :]
        for band in range(bands):
            index = (band // plane_count) * 8 + band % plane_count
            f_re, f_im = held[:, index : index + 1], held[:, 32 + index : 33 + index]
            row_n[band, pl.ds(start, 32), 0:M] = (f_re * ker_re - f_im * ker_im).astype(jnp.bfloat16)
            row_n[band, pl.ds(start, 32), M : 2 * M] = (f_re * ker_im + f_im * ker_re).astype(jnp.bfloat16)
        return carry

    slots = (half - 1) * groups
    done = 0
    for h in range(1, half):
        for g in range(groups):
            for way in range(2):
                if h <= hops(way, g):
                    gather_arrived(way, g, h - 1)
                    if h < hops(way, g):
                        gather_send(way, g, h)
            upto = ((h - 1) * groups + g + 1) * bands // slots
            if upto > done:
                lax.fori_loop(done, upto, build_lanes, 0)
                done = upto

    for g in range(groups):
        for way in range(2):
            if hops(way, g) == half:
                gather_arrived(way, g, half - 1)
        pupil_out[g] = jnp.dot(mix[...], coeff[g], preferred_element_type=jnp.float32).astype(jnp.bfloat16)
        mine = pl.ds(pl.multiple_of(me_r * span, span), span)
        for d, peer in enumerate(peers):
            theirs = pl.ds(pl.multiple_of(peer * span, span), span)
            send(pupil_out.at[g, theirs, :], pupil_in.at[g, mine, :], out_send.at[d, g], out_recv.at[d, g], (me_f, peer))
        pupil_in[g, mine, :] = pupil_out[g, mine, :]

    lax.fori_loop(0, size // 32, build_sublanes, 0)

    def source_of(d):
        dy, dx = steps[d]
        return ((y + y_count - dy) % y_count) * 2 + (x + 2 - dx) % 2

    for g in range(groups):
        for d in range(len(peers)):
            theirs = pl.ds(pl.multiple_of(source_of(d) * span, span), span)
            arrived(pupil_in.at[g, theirs, :], out_send.at[d, g], out_recv.at[d, g], (me_f, peers[d]))

        def forward(band, carry):
            base = pl.multiple_of(band * 2 * M, 2 * M)
            spectra = lax.dot_general(
                pupil_in[g], block_t[pl.ds(base, 2 * M), :], NT, preferred_element_type=jnp.float32
            ).astype(jnp.bfloat16)
            term = jnp.dot(
                row_t[pl.ds(base, 2 * M), g * slab : (g + 1) * slab], spectra, preferred_element_type=jnp.float32
            )
            image[band] = term if g == 0 else image[band] + term
            return carry

        lax.fori_loop(0, bands, forward, 0)

    def middle_step(band, carry):
        term = image[band]
        weight = wts[band]
        real = (weight * (term[:M, :M] - term[M:, M:])).astype(jnp.bfloat16)
        imag = (weight * (term[:M, M:] + term[M:, :M])).astype(jnp.bfloat16)
        square = jnp.concatenate(
            [jnp.concatenate([real, imag], axis=1), jnp.concatenate([imag, -real], axis=1)], axis=0
        )
        adjoint[:, pl.ds(pl.multiple_of(band * 2 * M, 2 * M), 2 * M)] = jnp.dot(
            row_n[band], square, preferred_element_type=jnp.float32
        ).astype(jnp.bfloat16)
        return carry

    lax.fori_loop(0, bands, middle_step, 0)

    def pull(g):
        def column(tile, carry):
            at = pl.ds(pl.multiple_of(tile * 256, 256), 256)
            pulled[g, :, at] = jnp.dot(
                adjoint[g * slab : (g + 1) * slab, :], block_t[:, at], preferred_element_type=jnp.float32
            ).astype(jnp.bfloat16)
            return carry

        lax.fori_loop(0, 2 * size // 256, column, 0)
        mine = pl.ds(pl.multiple_of(me_r * span, span), span)
        for d, peer in enumerate(peers):
            theirs = pl.ds(pl.multiple_of(peer * span, span), span)
            send(pulled.at[g, theirs, :], returned.at[g, mine, :], back_send.at[d, g], back_recv.at[d, g], (me_f, peer))
        returned[g, mine, :] = pulled[g, mine, :]

    def target(way, g, t):
        away = hops(way, g) - t
        return (z + away) % ring if way == 0 else (z + ring - away) % ring

    def rows_of(k):
        return pl.ds(pl.multiple_of(k * span, span), span)

    def scatter_slot(way, g, t, k):
        if way == 1 and t == hops(way, g) - 1:
            return partial_in.at[g, ring * span : (ring + 1) * span, :]
        return partial_in.at[g, rows_of(k), :]

    def scatter_send(way, g, t):
        k = target(way, g, t)
        send(
            part.at[g, rows_of(k), :], scatter_slot(way, g, t, k),
            rs_send.at[way, g, t], rs_recv.at[way, g, t], ring_to(way),
        )

    def scatter_arrived(way, g, t):
        k = target(way, g, t + 1) if t + 1 < hops(way, g) else z
        slot = scatter_slot(way, g, t, k)
        arrived(slot, rs_send.at[way, g, t], rs_recv.at[way, g, t], ring_to(way))
        return k

    def collect(g):
        for d in range(len(peers)):
            theirs = rows_of(source_of(d))
            arrived(returned.at[g, theirs, :], back_send.at[d, g], back_recv.at[d, g], (me_f, peers[d]))
        part[g] = jnp.dot(mix_t[...], returned[g], preferred_element_type=jnp.float32)
        for way in range(2):
            scatter_send(way, g, 0)

    def advance(g, t):
        for way in range(2):
            if t < hops(way, g):
                k = scatter_arrived(way, g, t - 1)
                part[g, rows_of(k), :] = part[g, rows_of(k), :] + partial_in[g, rows_of(k), :]
                scatter_send(way, g, t)

    factor = 4.0 / (bands * total_slits)

    def finish(g):
        for way in range(2):
            scatter_arrived(way, g, hops(way, g) - 1)
        total = part[g, rows_of(z), :] + partial_in[g, rows_of(z), :]
        total = (total + partial_in[g, ring * span : (ring + 1) * span, :]) * factor
        mask = support[g * span : (g + 1) * span, :].astype(jnp.float32)
        for c in range(2):
            out[0, c, g * span : (g + 1) * span, :] = total[:, c * size : (c + 1) * size] * mask

    pull(0)
    pull(1)
    for slot in range(groups + half):
        if slot < groups:
            collect(slot)
        if slot + 2 < groups:
            pull(slot + 2)
        for t in range(1, half):
            if 0 <= slot - t < groups:
                advance(slot - t, t)
        if 0 <= slot - half < groups:
            finish(slot - half)

    for copy in sent:
        copy.wait_send()


def local(direction, slits, sources, support, focus, slit_focus, obj_rows, obj_cols, weights):
    row_count = lax.axis_size("row")
    ring = lax.axis_size("field") // J
    size = direction.shape[3]
    src_count, plane_count = sources.shape[0], focus.shape[0]
    bands = src_count * plane_count
    span = size // (row_count * GROUPS)
    slab = span * row_count
    total_slits = slits.shape[0] * lax.axis_size("field")
    cols_t, rows_t, rows = kernel_tables(size, row_count, GROUPS)
    smem = pl.BlockSpec(memory_space=pltpu.SMEM)
    vmem = pl.BlockSpec(memory_space=pltpu.VMEM)
    hbm = pl.BlockSpec(memory_space=pl.ANY)
    dma = pltpu.SemaphoreType.DMA
    half = ring // 2
    peers = row_count - 1
    return pl.pallas_call(
        functools.partial(body, (ring, row_count, src_count, plane_count, size, total_slits)),
        out_shape=jax.ShapeDtypeStruct(direction.shape, jnp.float32),
        in_specs=[smem, smem, smem, smem, vmem, vmem, vmem, vmem, hbm, hbm, hbm, hbm],
        out_specs=vmem,
        scratch_shapes=[
            pltpu.VMEM(cols_t.shape, jnp.float32),
            pltpu.VMEM(rows_t.shape, jnp.float32),
            pltpu.VMEM(rows.shape, jnp.float32),
            pltpu.VMEM((bands, M, M), jnp.float32),
            pltpu.VMEM((J, 4 * span, 128), jnp.float32),
            pltpu.VMEM((GROUPS, ring * span, 2 * size), jnp.bfloat16),
            pltpu.VMEM((slab, ring * span), jnp.bfloat16),
            pltpu.VMEM((ring * span, slab), jnp.bfloat16),
            pltpu.VMEM((128, size), jnp.float32),
            pltpu.VMEM((size, 128), jnp.float32),
            pltpu.VMEM((128, size), jnp.float32),
            pltpu.VMEM((bands * 2 * M, 2 * size), jnp.bfloat16),
            pltpu.VMEM((bands * 2 * M, size), jnp.bfloat16),
            pltpu.VMEM((bands, size, 2 * M), jnp.bfloat16),
            pltpu.VMEM((GROUPS, slab, 2 * size), jnp.bfloat16),
            pltpu.VMEM((GROUPS, slab, 2 * size), jnp.bfloat16),
            pltpu.VMEM((bands, 2 * M, 2 * M), jnp.float32),
            pltpu.VMEM((size, bands * 2 * M), jnp.bfloat16),
            pltpu.VMEM((GROUPS, slab, 2 * size), jnp.bfloat16),
            pltpu.VMEM((GROUPS, slab, 2 * size), jnp.bfloat16),
            pltpu.VMEM((GROUPS, ring * span, 2 * size), jnp.float32),
            pltpu.VMEM((GROUPS, (ring + 1) * span, 2 * size), jnp.float32),
            dma((4,)),
            dma((J - 1,)),
            dma((J - 1,)),
            dma((2, GROUPS, half)),
            dma((2, GROUPS, half)),
            dma((peers, GROUPS)),
            dma((peers, GROUPS)),
            dma((peers, GROUPS)),
            dma((peers, GROUPS)),
            dma((2, GROUPS, half)),
            dma((2, GROUPS, half)),
        ],
        compiler_params=pltpu.CompilerParams(
            collective_id=0, has_side_effects=True, vmem_limit_bytes=56 * 1024 * 1024
        ),
    )(
        slits, sources, focus, slit_focus, direction, support, obj_rows, obj_cols,
        weights.reshape(bands, M, M), cols_t, rows_t, rows,
    )


def solution(mesh):
    return jax.shard_map(
        local,
        mesh=mesh,
        in_specs=(
            P("field", None, "row", None),
            P("field"),
            P(),
            P("row", None),
            P(),
            P("field"),
            P(),
            P(),
            P(),
        ),
        out_specs=P("field", None, "row", None),
        check_vma=False,
    )
```

time: 477 us -> 98.5 us (0.21)
  waiting for transfers between devices: 173 us -> 0 us
  other arithmetic: 127 us -> 0 us
  Pallas kernels: 0 us -> 95.3 us
  local copies, waits for them, and re-layouts: 80 us -> 1.67 us
  blocking collectives: 41.1 us -> 0 us
  matrix products: 32.4 us -> 0 us
  between operations: 13.8 us -> 0.01 us
  starting transfers between devices: 6.06 us -> 0 us
    reduce_scatter x1 -> x0, waiting for transfers between devices: 154 us -> none  [local(): lax.psum_scatter(jnp.einsum('sjt,sjrcn->tcrn', chosen, pulled, preferred_...]
    pallas_call x0 -> x1, Pallas kernels: none -> 95.3 us  [local(): pl.pallas_call(functools.partial(body, (ring, row_count, src_count, plane...]
    another operation x7 -> x0, other arithmetic: 54.5 us -> none  [the longest x2 50.6 us: tables(): block = jnp.stack([upper, lower], axis=3)]
    all_to_all x1 -> x0, blocking collectives: 41.1 us -> none  [local(): lax.all_to_all(adjoint, 'row', split_axis=2, concat_axis=0, tiled=True)]
    convert_element_type x5 -> x0, other arithmetic: 34.7 us -> none  [the longest x2 34.6 us: apply(): return (real_part.astype(jnp.bfloat16), imag_part.astype(jnp.bfloat16))]
    dot_general x9 -> x0, matrix products: 32.4 us -> none  [the longest x1 9.35 us: local(): jnp.einsum('sjrc,sqzcy->sjqzry', pupil_four, block, preferred_element_typ...]
    neg x1 -> x0, other arithmetic: 28.5 us -> none  [tables(): lower = jnp.stack([-map_im, map_re], axis=4)]
    reshape x2 -> x0, local copies, waits for them, and re-layouts: 23.6 us -> none  [the longest x1 20.5 us: tables(): block.reshape(block.shape[0], block.shape[1], block.shape[2], 2 * N, 2 * M)]
  transfers between devices with their start and end apart: 3 -> 0, of which waited for: 2 -> 0; matrix products, arithmetic and copies ran while one was open for 34% -> 0% of each run, Pallas kernels for 0% -> 0%
where the time goes in v1:
time: 98.5 us; the launch traced here: 97 us
  Pallas kernels  95.3 us (97%)
  local copies, waits for them, and re-layouts  1.67 us (2%)
    pallas_call x1, Pallas kernels, local(): pl.pallas_call(functools.partial(body, (ring, row_count, src_count, plane...  95.3 us

profile of v1, /device:TPU:6, one launch (start us, length us, event | category | flops | bytes accessed | tf_op | source)
XLA Modules:
  0.0 97.0 jit_solution(6439241506205488533)
XLA Ops:
  0.0 95.3 %shard_map.118 = f32[1,2,64,512]{3,2,1,0:T(8,128)} custom-call(s32[2]{0:T(128)} %slits.1, s32[4]{0:T(128)} %sources.1, f32[3]{0:T(128)} %focus.1, f32[2]{0:T(128)} %slit_focus.1, bf16[1,2,64,512]{3,2,1,0:T(8,128)(2,1)} %direction.1, s32[64,512]{1,0:T(8,128)} %support.1, f32[2,576]{1,0:T(2,128)} %obj_rows.1, f32[2,576]{1,0:T(2,128)} %obj_cols.1, ...), custom_call_target="tpu_custom_call" | custom-call | tf_op jit(solution)/shard_map/pallas_call | solution.py:362
  95.3 1.7 %copy.14 = f32[1,2,64,512]{3,2,1,0:T(8,128)} copy(f32[1,2,64,512]{3,2,1,0:T(8,128)} %shard_map.118) | data formatting | bytes 524288

commit v2 on v1

v2 whole, which is shorter than its diff:
```python
import functools
import math

import jax
import jax.numpy as jnp
import numpy as np
from jax import lax
from jax.experimental import pallas as pl
from jax.experimental.pallas import tpu as pltpu
from jax.sharding import PartitionSpec as P

J = 4
M = 128
SLIT_GRID = 512
SRC_SIDE = 9
SHIFT = 8
PAD = 32
GROUPS = 4
LEVELS = 32000.0
MESH = pl.DeviceIdType.MESH


def kernel_tables(size, blocks, groups):
    freq = np.arange(size)
    span = size // (blocks * groups)
    order = freq.reshape(blocks, groups, span).transpose(1, 0, 2).reshape(-1)

    def kernel(stretch):
        turns = np.mod(stretch * (freq - size // 2)[:, None] * (np.arange(M) - M // 2)[None, :], size)
        angle = (turns.astype(np.float32) * np.float32(-2.0 * math.pi / size)).astype(np.float64)
        scale = 1.0 / math.sqrt(M)
        return np.stack([np.cos(angle) * scale, np.sin(angle) * scale]).astype(np.float32)

    last = np.stack([kernel(1), kernel(2)[:, order]])
    return np.ascontiguousarray(last.transpose(0, 1, 3, 2)), last


def body(sizes, slits, sources, focus, slit_focus, direction_hbm, support_hbm, obj_rows_hbm, obj_cols_hbm, weights_hbm,
         ker_t_hbm, ker_n_hbm, out_hbm,
         direction, support, obj_rows, obj_cols, weights, ker_t, ker_n, info, coeff, mix, mix_t, pick, fac, fac_c, fac_t, fac_p,
         col_t, row_t, col_n, row_n, pupil_out, pupil_in, spec, image, adj_re, adj_im, pulled, returned, part, part_out, part_in, out,
         load_sem, out_sem, info_send, info_recv, ag_send, ag_recv, out_send, out_recv, back_send, back_recv, rs_send, rs_recv):
    ring, row_count, src_count, plane_count, size, total_slits = sizes
    groups = GROUPS
    span = size // (row_count * groups)
    slab = span * row_count
    bands = src_count * plane_count
    half = ring // 2
    me_f, me_r = lax.axis_index("field"), lax.axis_index("row")
    z, j = me_f // J, me_f % J
    y, x = me_r // 2, me_r % 2
    y_count = row_count // 2
    right = (((z + 1) % ring) * J + j, me_r)
    left = (((z + ring - 1) % ring) * J + j, me_r)
    siblings = [(z * J + (j + d) % J, me_r) for d in range(1, J)]
    steps = [(dy, dx) for dy in (2, 1, 3, 0) for dx in (1, 0) if dy < y_count and (dy, dx) != (0, 0)]
    peers = [((y + dy) % y_count) * 2 + (x + dx) % 2 for dy, dx in steps]

    barrier = pltpu.get_barrier_semaphore()
    greeted = [right, left] + siblings + [(me_f, peer) for peer in peers]
    for device in greeted:
        pl.semaphore_signal(barrier, inc=1, device_id=device, device_id_type=MESH)

    loads = [
        pltpu.make_async_copy(src, dst, load_sem.at[i])
        for i, (src, dst) in enumerate(
            [(direction_hbm, direction), (support_hbm, support), (obj_rows_hbm, obj_rows), (obj_cols_hbm, obj_cols),
             (ker_t_hbm, ker_t), (ker_n_hbm, ker_n), (weights_hbm, weights)]
        )
    ]
    for load in loads:
        load.start()

    def rows_of(k, g=0):
        return pl.ds(pl.multiple_of(g * slab + k * span, span), span)

    def group(g):
        return slice(g * slab, (g + 1) * slab)

    for i in range(2):
        position = (2.0 * slits[i].astype(jnp.float32) + 1.0) / SLIT_GRID - 1.0
        info[j, i * span : (i + 1) * span, :] = jnp.full((span, 128), position, jnp.float32)
        info[j, (2 + i) * span : (3 + i) * span, :] = jnp.full((span, 128), slit_focus[i], jnp.float32)
    loads[0].wait()
    for g in range(groups):
        for c in range(2):
            coeff[rows_of(z, g), c * size : (c + 1) * size] = direction[0, c, g * span : (g + 1) * span, :]

    pl.semaphore_wait(barrier, len(greeted))

    def send(src, dst, send_sem, recv_sem, device):
        copy = pltpu.make_async_remote_copy(
            src_ref=src, dst_ref=dst, send_sem=send_sem, recv_sem=recv_sem, device_id=device, device_id_type=MESH
        )
        copy.start()

    def arrived(dst, send_sem, recv_sem, device):
        pltpu.make_async_remote_copy(
            src_ref=dst, dst_ref=dst, send_sem=send_sem, recv_sem=recv_sem, device_id=device, device_id_type=MESH
        ).wait_recv()

    def hops(way, g):
        return half if way == g % 2 else half - 1

    def ring_to(way):
        return right if way == 0 else left

    def gather_slot(way, g, h):
        k = (z + ring - h) % ring if way == 0 else (z + h) % ring
        return coeff.at[rows_of(k, g), :]

    def gather_send(way, g, h):
        slot = gather_slot(way, g, h)
        send(slot, slot, ag_send.at[0], ag_recv.at[way, g, h], ring_to(way))

    def gather_arrived(way, g, h):
        arrived(gather_slot(way, g, h + 1), ag_send.at[0], ag_recv.at[way, g, h], ring_to(way))

    def windows():
        for load in loads[2:4]:
            load.wait()
        middle = SRC_SIDE // 2
        for axis, spectrum in enumerate((obj_rows, obj_cols)):
            shifted = [spectrum[:, PAD - SHIFT * (v - middle) : PAD - SHIFT * (v - middle) + size] for v in range(SRC_SIDE)]
            for q in range(src_count):
                place = sources[q] // SRC_SIDE if axis == 0 else sources[q] % SRC_SIDE
                picked = shifted[0]
                for v in range(1, SRC_SIDE):
                    picked = jnp.where(place == v, shifted[v], picked)
                pick[axis, 8 * q : 8 * q + 2, :] = picked

    def phases():
        own_focus = info[me_r // 2, pl.ds((2 + me_r % 2) * span, 8), :]
        own_focus = jnp.concatenate([own_focus] * (size // 128), axis=1)
        which = lax.broadcasted_iota(jnp.int32, (8, size), 0)
        plane = jnp.full((8, size), focus[0], jnp.float32)
        for p in range(1, plane_count):
            plane = jnp.where(which == p, focus[p], plane)
        freq = lax.broadcasted_iota(jnp.int32, (8, size), 1)
        scaled = (2 * freq - size + 1).astype(jnp.float32) / size
        theta = math.pi * (plane + own_focus) * (scaled * scaled)
        return jnp.cos(theta), jnp.sin(theta)

    def factors(q, turn_cos, turn_sin):
        for axis in range(2):
            first, second = pick[axis, 8 * q : 8 * q + 1, :], pick[axis, 8 * q + 1 : 8 * q + 2, :]
            base = 64 * axis + 8 * q
            fac[base : base + 8, :] = first * turn_cos - second * turn_sin
            fac[base + 32 : base + 40, :] = first * turn_sin + second * turn_cos

    def turn_factors():
        fac_c[...] = fac[...].T
        for g in range(groups):
            for r in range(row_count):
                start = r * groups * span + g * span
                fac_t[g * slab + r * span : g * slab + (r + 1) * span, :] = fac_c[start : start + span, :]
        fac_p[...] = fac_t[...].T

    def mixing():
        edge = row_count * span
        position = jnp.concatenate([info[s, 0 : 2 * span, :] for s in range(J)], axis=0)
        position = jnp.concatenate([position] * (edge // 128), axis=1) if edge > 128 else position
        sub = lax.broadcasted_iota(jnp.int32, (edge, edge), 0)
        lane = lax.broadcasted_iota(jnp.int32, (edge, edge), 1)
        before, now = jnp.ones_like(position), position
        chosen = jnp.where(lane // span == 0, before, jnp.where(lane // span == 1, now, 0.0))
        for order in range(1, ring - 1):
            before, now = now, ((2.0 * order + 1.0) * position * now - order * before) / (order + 1.0)
            chosen = jnp.where(lane // span == order + 1, now, chosen)
        chosen = jnp.where(sub % span == lane % span, chosen, 0.0)
        mix[...] = chosen.astype(jnp.bfloat16)
        mix_t[...] = chosen.T.astype(jnp.bfloat16)

    def index_of(band):
        return (band // plane_count) * 8 + band % plane_count

    def build_lanes(band, carry):
        index = index_of(band)
        cf_re, cf_im = fac[pl.ds(64 + index, 1), :], fac[pl.ds(96 + index, 1), :]
        rf_re, rf_im = fac_p[pl.ds(index, 1), :], fac_p[pl.ds(32 + index, 1), :]
        col_base, row_base = pl.multiple_of(band * M, M), pl.multiple_of(band * 2 * M, 2 * M)
        for m in range(0, M, 16):
            ker_re, ker_im = ker_t[0, 0, m : m + 16, :], ker_t[0, 1, m : m + 16, :]
            col_t[pl.ds(col_base + m, 16), 0:size] = (cf_re * ker_re - cf_im * ker_im).astype(jnp.bfloat16)
            col_t[pl.ds(col_base + m, 16), size : 2 * size] = (cf_re * ker_im + cf_im * ker_re).astype(jnp.bfloat16)
            ker_re, ker_im = ker_t[1, 0, m : m + 16, :], ker_t[1, 1, m : m + 16, :]
            row_t[pl.ds(row_base + m, 16), :] = (rf_re * ker_re - rf_im * ker_im).astype(jnp.bfloat16)
            row_t[pl.ds(row_base + M + m, 16), :] = (rf_re * ker_im + rf_im * ker_re).astype(jnp.bfloat16)
        return carry

    def build_sublanes(axis, held, offset, table):
        def step(i, carry):
            at = pl.ds(pl.multiple_of(i * 32, 32), 32)
            ker_re, ker_im = ker_n[axis, 0, at, :], ker_n[axis, 1, at, :]
            values = held[at, :]
            for band in range(bands):
                index = offset + index_of(band)
                f_re, f_im = values[:, index : index + 1], values[:, 32 + index : 33 + index]
                table[band, at, 0:M] = (f_re * ker_re - f_im * ker_im).astype(jnp.bfloat16)
                table[band, at, M : 2 * M] = (f_re * ker_im + f_im * ker_re).astype(jnp.bfloat16)
            return carry

        return step

    build_col = build_sublanes(0, fac_c, 64, col_n)
    build_row = build_sublanes(1, fac_t, 0, row_n)
    slices = size // 32

    def start_tables():
        for d in range(J - 1):
            arrived(info.at[(j + J - 1 - d) % J], info_send.at[0], info_recv.at[d], siblings[d])
        turn_cos, turn_sin = phases()
        for q in range(src_count):
            factors(q, turn_cos, turn_sin)
        turn_factors()
        mixing()
        for load in loads[4:6]:
            load.wait()

    def own(g):
        for way in range(2):
            gather_send(way, g, 0)

    def relay(g, h):
        for way in range(2):
            if h <= hops(way, g):
                gather_arrived(way, g, h - 1)
                if h < hops(way, g):
                    gather_send(way, g, h)

    def masked(values, g):
        mask = support[g * span : (g + 1) * span, :].astype(jnp.float32)
        mask = jnp.concatenate([mask, mask], axis=1)
        return values * jnp.concatenate([mask] * (values.shape[0] // span), axis=0)

    def pupils(g):
        relay(g, half)
        summed = jnp.dot(mix[...], coeff[group(g), :], preferred_element_type=jnp.float32)
        pupil_out[group(g), :] = masked(summed, g).astype(jnp.bfloat16)
        for d, peer in enumerate(peers):
            send(
                pupil_out.at[rows_of(peer, g), :], pupil_in.at[rows_of(me_r, g), :],
                out_send.at[0], out_recv.at[g], (me_f, peer),
            )
        pupil_in[rows_of(me_r, g), :] = pupil_out[rows_of(me_r, g), :]

    def build(step, first, last, parts, count):
        lax.fori_loop(first * count // parts, last * count // parts, step, 0)

    for g in range(groups):
        own(g)
    for d, device in enumerate(siblings):
        send(info.at[j], info.at[j], info_send.at[0], info_recv.at[d], device)
    windows()
    cols = 0
    for h in range(1, half):
        for g in range(groups):
            relay(g, h)
            if (h, g) == (1, groups - 1):
                start_tables()
                loads[1].wait()
            if h > 1:
                build(build_col, cols, cols + 1, 2 * groups, slices)
                cols += 1
    build(build_lanes, 0, 1, 2, bands)
    for g in range(groups):
        pupils(g)
    build(build_lanes, 1, 2, 2, bands)

    def exchanged(landed, send_sem, recv_sem, g):
        blocks = landed.at[g * slab : g * slab + len(peers) * span, :]
        arrived(blocks, send_sem.at[0], recv_sem.at[g], (me_f, peers[0]))

    def spectra_of(g, band):
        stacked = jnp.concatenate([pupil_in[group(g), 0:size], pupil_in[group(g), size : 2 * size]], axis=0)
        prod = jnp.dot(stacked, col_n[band], preferred_element_type=jnp.float32)
        real = prod[:slab, :M] - prod[slab:, M:]
        imag = prod[:slab, M:] + prod[slab:, :M]
        return jnp.concatenate([real, imag], axis=1).astype(jnp.bfloat16)

    def spectra(g):
        exchanged(pupil_in, out_send, out_recv, g)

        def step(band, carry):
            spec[band, g % 2 * slab : (g % 2 + 1) * slab, :] = spectra_of(g, band)
            return carry

        lax.fori_loop(0, bands, step, 0, unroll=True)

    def images(g):
        def step(band, carry):
            base = pl.multiple_of(band * 2 * M, 2 * M)
            kernel = row_t[pl.ds(base, 2 * M), g * slab : (g + 2) * slab]
            term = jnp.dot(kernel, spec[band], preferred_element_type=jnp.float32)
            image[band] = term if g == 0 else image[band] + term
            return carry

        lax.fori_loop(0, bands, step, 0, unroll=True)

    def adjoints():
        def step(band, carry):
            term = image[band]
            weight = weights[band]
            real = (weight * (term[:M, :M] - term[M:, M:])).astype(jnp.bfloat16)
            imag = (weight * (term[:M, M:] + term[M:, :M])).astype(jnp.bfloat16)
            square = jnp.concatenate(
                [jnp.concatenate([real, imag], axis=1), jnp.concatenate([imag, -real], axis=1)], axis=0
            )
            back = jnp.dot(row_n[band], square, preferred_element_type=jnp.float32).astype(jnp.bfloat16)
            at = pl.ds(pl.multiple_of(band * M, M), M)
            adj_re[:, at] = back[:, :M]
            adj_im[:, at] = back[:, M:]
            return carry

        lax.fori_loop(0, bands, step, 0, unroll=True)

    spectra(0)
    build(build_row, 0, 1, 2, slices)
    spectra(1)
    images(0)
    build(build_row, 1, 2, 2, slices)
    loads[6].wait()
    spectra(2)
    spectra(3)
    images(2)
    adjoints()

    def pull(g):
        rows = slice(g * slab, (g + 1) * slab)
        stacked = jnp.concatenate([adj_re[rows, :], adj_im[rows, :]], axis=0)
        with_re = jnp.dot(stacked, col_t[:, 0:size], preferred_element_type=jnp.float32)
        with_im = jnp.dot(stacked, col_t[:, size : 2 * size], preferred_element_type=jnp.float32)
        pulled[group(g), 0:size] = (with_re[:slab] + with_im[slab:]).astype(jnp.bfloat16)
        pulled[group(g), size : 2 * size] = (with_re[slab:] - with_im[:slab]).astype(jnp.bfloat16)
        for d, peer in enumerate(peers):
            send(
                pulled.at[rows_of(peer, g), :], returned.at[rows_of(me_r, g), :],
                back_send.at[0], back_recv.at[g], (me_f, peer),
            )
        returned[rows_of(me_r, g), :] = pulled[rows_of(me_r, g), :]

    def target(way, g, t):
        away = hops(way, g) - t
        return (z + away) % ring if way == 0 else (z + ring - away) % ring

    def scatter_slot(way, g, t, k):
        if way == 1 and t == hops(way, g) - 1:
            return part_in.at[g, ring * span : (ring + 1) * span, :]
        return part_in.at[g, rows_of(k), :]

    def coded(values):
        top = jnp.max(jnp.abs(values), axis=1, keepdims=True)
        power = jnp.ceil(jnp.log2(jnp.maximum(jnp.broadcast_to(top, (span, 128)), 2.0**-120)))
        scale = jnp.concatenate([jnp.exp2(-power)] * (2 * size // 128), axis=1)
        levels = jnp.round(values * scale * LEVELS)
        return levels.astype(jnp.int32).astype(jnp.int16), power.astype(jnp.int32).astype(jnp.int16)

    def decoded(slot):
        power = slot[:, 2 * size :].astype(jnp.int32).astype(jnp.float32)
        scale = jnp.concatenate([jnp.exp2(power) * (1.0 / LEVELS)] * (2 * size // 128), axis=1)
        return slot[:, 0 : 2 * size].astype(jnp.int32).astype(jnp.float32) * scale

    def scatter_send(way, g, t):
        k = target(way, g, t)
        levels, power = coded(part[rows_of(k, g), :])
        part_out[rows_of(k, g), 0 : 2 * size] = levels
        part_out[rows_of(k, g), 2 * size :] = power
        send(
            part_out.at[rows_of(k, g), :], scatter_slot(way, g, t, k),
            rs_send.at[0], rs_recv.at[way, g, t], ring_to(way),
        )

    def scatter_arrived(way, g, t):
        k = target(way, g, t + 1) if t + 1 < hops(way, g) else z
        slot = scatter_slot(way, g, t, k)
        arrived(slot, rs_send.at[0], rs_recv.at[way, g, t], ring_to(way))
        return k

    def collect(g):
        exchanged(returned, back_send, back_recv, g)
        part[group(g), :] = jnp.dot(mix_t[...], returned[group(g), :], preferred_element_type=jnp.float32)
        for way in range(2):
            scatter_send(way, g, 0)

    def advance(g, t):
        for way in range(2):
            if t < hops(way, g):
                k = scatter_arrived(way, g, t - 1)
                part[rows_of(k, g), :] = part[rows_of(k, g), :] + decoded(part_in.at[g, rows_of(k), :])
                scatter_send(way, g, t)

    factor = 4.0 / (bands * total_slits)
    leaving = []

    def finish(g):
        for way in range(2):
            scatter_arrived(way, g, hops(way, g) - 1)
        total = part[rows_of(z, g), :] + decoded(part_in.at[g, rows_of(z), :])
        total = (total + decoded(part_in.at[g, ring * span : (ring + 1) * span, :])) * factor
        total = masked(total, g)
        for c in range(2):
            out[g, c] = total[:, c * size : (c + 1) * size]
        leave = pltpu.make_async_copy(out.at[g], out_hbm.at[0, :, g * span : (g + 1) * span, :], out_sem.at[g])
        leave.start()
        leaving.append(leave)

    for g in range(groups):
        pull(g)
    for slot in range(groups + half):
        if slot < groups:
            collect(slot)
        for t in range(1, half):
            if 0 <= slot - t < groups:
                advance(slot - t, t)
        if 0 <= slot - half < groups:
            finish(slot - half)

    rounds = (ring - 1) * groups * span
    for moved, count, sem in (
        (info, J - 1, info_send), (coeff, rounds, ag_send), (pupil_out, len(peers) * groups * span, out_send),
        (pulled, len(peers) * groups * span, back_send), (part_out, rounds, rs_send),
    ):
        all_sent = moved.at[0:count]
        pltpu.make_async_remote_copy(
            src_ref=all_sent, dst_ref=all_sent, send_sem=sem.at[0], recv_sem=sem.at[0], device_id=right, device_id_type=MESH
        ).wait_send()
    for leave in leaving:
        leave.wait()


def local(direction, slits, sources, support, focus, slit_focus, obj_rows, obj_cols, weights):
    row_count = lax.axis_size("row")
    ring = lax.axis_size("field") // J
    size = direction.shape[3]
    src_count, plane_count = sources.shape[0], focus.shape[0]
    bands = src_count * plane_count
    span = size // (row_count * GROUPS)
    slab = span * row_count
    total_slits = slits.shape[0] * lax.axis_size("field")
    ker_t, ker_n = kernel_tables(size, row_count, GROUPS)
    weights = weights.reshape(bands, M, M)
    smem = pl.BlockSpec(memory_space=pltpu.SMEM)
    hbm = pl.BlockSpec(memory_space=pl.ANY)
    dma = pltpu.SemaphoreType.DMA
    half = ring // 2
    peers = row_count - 1
    f32, bf16 = jnp.float32, jnp.bfloat16
    return pl.pallas_call(
        functools.partial(body, (ring, row_count, src_count, plane_count, size, total_slits)),
        out_shape=jax.ShapeDtypeStruct(direction.shape, jnp.float32),
        in_specs=[smem] * 4 + [hbm] * 7,
        out_specs=hbm,
        scratch_shapes=[
            pltpu.VMEM(direction.shape, bf16),
            pltpu.VMEM(support.shape, jnp.int32),
            pltpu.VMEM(obj_rows.shape, f32),
            pltpu.VMEM(obj_cols.shape, f32),
            pltpu.VMEM(weights.shape, f32),
            pltpu.VMEM(ker_t.shape, f32),
            pltpu.VMEM(ker_n.shape, f32),
            pltpu.VMEM((J, 4 * span, 128), f32),
            pltpu.VMEM((GROUPS * ring * span, 2 * size), bf16),
            pltpu.VMEM((slab, ring * span), bf16),
            pltpu.VMEM((ring * span, slab), bf16),
            pltpu.VMEM((2, 8 * src_count, size), f32),
            pltpu.VMEM((128, size), f32),
            pltpu.VMEM((size, 128), f32),
            pltpu.VMEM((size, 128), f32),
            pltpu.VMEM((128, size), f32),
            pltpu.VMEM((bands * M, 2 * size), bf16),
            pltpu.VMEM((bands * 2 * M, size), bf16),
            pltpu.VMEM((bands, size, 2 * M), bf16),
            pltpu.VMEM((bands, size, 2 * M), bf16),
            pltpu.VMEM((GROUPS * slab, 2 * size), bf16),
            pltpu.VMEM((GROUPS * slab, 2 * size), bf16),
            pltpu.VMEM((bands, 2 * slab, 2 * M), bf16),
            pltpu.VMEM((bands, 2 * M, 2 * M), f32),
            pltpu.VMEM((size, bands * M), bf16),
            pltpu.VMEM((size, bands * M), bf16),
            pltpu.VMEM((GROUPS * slab, 2 * size), bf16),
            pltpu.VMEM((GROUPS * slab, 2 * size), bf16),
            pltpu.VMEM((GROUPS * ring * span, 2 * size), f32),
            pltpu.VMEM((GROUPS * ring * span, 2 * size + 128), jnp.int16),
            pltpu.VMEM((GROUPS, (ring + 1) * span, 2 * size + 128), jnp.int16),
            pltpu.VMEM((GROUPS, 2, span, size), f32),
            dma((7,)),
            dma((GROUPS,)),
            dma((1,)),
            dma((J - 1,)),
            dma((1,)),
            dma((2, GROUPS, half)),
            dma((1,)),
            dma((GROUPS,)),
            dma((1,)),
            dma((GROUPS,)),
            dma((1,)),
            dma((2, GROUPS, half)),
        ],
        compiler_params=pltpu.CompilerParams(
            collective_id=0, has_side_effects=True, vmem_limit_bytes=56 * 1024 * 1024
        ),
    )(slits, sources, focus, slit_focus, direction, support, obj_rows, obj_cols, weights, ker_t, ker_n)


def solution(mesh):
    return jax.shard_map(
        local,
        mesh=mesh,
        in_specs=(
            P("field", None, "row", None),
            P("field"),
            P(),
            P("row", None),
            P(),
            P("field"),
            P(),
            P(),
            P(),
        ),
        out_specs=P("field", None, "row", None),
        check_vma=False,
    )
```

time: 98.5 us -> 68.8 us (0.70)
  the two profiles are of different devices: /device:TPU:6 before, /device:TPU:34 now
where the time goes in v2:
time: 68.8 us; the launch traced here: 68.7 us
  Pallas kernels  67 us (97%)
  local copies, waits for them, and re-layouts  1.67 us (2%)
    pallas_call x1, Pallas kernels, local(): pl.pallas_call(functools.partial(body, (ring, row_count, src_count, plane...  67 us
    unnamed x1, local copies, waits for them, and re-layouts  1.67 us

profile of v2, /device:TPU:34, one launch (start us, length us, event | category | flops | bytes accessed | tf_op | source)
XLA Modules:
  0.0 68.7 jit_solution(12922128492448712944)
XLA Ops:
  0.0 67.0 %shard_map.109 = f32[1,2,64,512]{3,2,1,0:T(8,128)} custom-call(s32[2]{0:T(128)} %slits.1, s32[4]{0:T(128)} %sources.1, f32[3]{0:T(128)} %focus.1, f32[2]{0:T(128)} %slit_focus.1, bf16[1,2,64,512]{3,2,1,0:T(8,128)(2,1)} %direction_hbm.1, s32[64,512]{1,0:T(8,128)} %support_hbm.1, f32[2,576]{1,0:T(2,128)} %obj_rows_hbm.1, f32[2,576]{1,0:T(2,128)} %obj_cols_hbm.1, ...), custom_call_target="tpu_custom_call" | custom-call | tf_op jit(solution)/shard_map/pallas_call | solution.py:448
  67.0 1.7 %copy.13 = f32[1,2,64,512]{3,2,1,0:T(8,128)} copy(f32[1,2,64,512]{3,2,1,0:T(8,128)} %shard_map.109) | data formatting | bytes 524288

commit v3 on v2

--- a/solution.py
+++ b/solution.py
@@ -40,7 +40,7 @@
          direction, support, obj_rows, obj_cols, weights, ker_t, ker_n, info, coeff, mix, mix_t, pick, fac, fac_c, fac_t, fac_p,
          col_t, row_t, col_n, row_n, pupil_out, pupil_in, spec, image, adj_re, adj_im, pulled, returned, part, part_out, part_in, out,
          load_sem, out_sem, info_send, info_recv, ag_send, ag_recv, out_send, out_recv, back_send, back_recv, rs_send, rs_recv):
-    ring, row_count, src_count, plane_count, size, total_slits = sizes
+    ring, row_count, src_count, plane_count, size = sizes
     groups = GROUPS
     span = size // (row_count * groups)
     slab = span * row_count
@@ -50,14 +50,20 @@
     z, j = me_f // J, me_f % J
     y, x = me_r // 2, me_r % 2
     y_count = row_count // 2
-    right = (((z + 1) % ring) * J + j, me_r)
-    left = (((z + ring - 1) % ring) * J + j, me_r)
+
+    def ahead(way, n):
+        return (z + n) % ring if way == 0 else (z + ring - n) % ring
+
+    def ring_to(way, n=1):
+        return (ahead(way, n) * J + j, me_r)
+
+    right = ring_to(0)
     siblings = [(z * J + (j + d) % J, me_r) for d in range(1, J)]
     steps = [(dy, dx) for dy in (2, 1, 3, 0) for dx in (1, 0) if dy < y_count and (dy, dx) != (0, 0)]
     peers = [((y + dy) % y_count) * 2 + (x + dx) % 2 for dy, dx in steps]
 
     barrier = pltpu.get_barrier_semaphore()
-    greeted = [right, left] + siblings + [(me_f, peer) for peer in peers]
+    greeted = [ring_to(way, n) for way in range(2) for n in (1, 2, 3)] + siblings + [(me_f, peer) for peer in peers]
     for device in greeted:
         pl.semaphore_signal(barrier, inc=1, device_id=device, device_id_type=MESH)
 
@@ -99,22 +105,18 @@
             src_ref=dst, dst_ref=dst, send_sem=send_sem, recv_sem=recv_sem, device_id=device, device_id_type=MESH
         ).wait_recv()
 
-    def hops(way, g):
-        return half if way == g % 2 else half - 1
-
-    def ring_to(way):
-        return right if way == 0 else left
-
-    def gather_slot(way, g, h):
-        k = (z + ring - h) % ring if way == 0 else (z + h) % ring
-        return coeff.at[rows_of(k, g), :]
-
-    def gather_send(way, g, h):
-        slot = gather_slot(way, g, h)
-        send(slot, slot, ag_send.at[0], ag_recv.at[way, g, h], ring_to(way))
-
-    def gather_arrived(way, g, h):
-        arrived(gather_slot(way, g, h + 1), ag_send.at[0], ag_recv.at[way, g, h], ring_to(way))
+    def long_way(g):
+        return g % 2
+
+    def gather_slot(way, g, distance):
+        return coeff.at[rows_of(ahead(1 - way, distance), g), :]
+
+    def gather_send(way, g, distance, n=1):
+        slot = gather_slot(way, g, distance)
+        send(slot, slot, ag_send.at[0], ag_recv.at[way, g, distance + n - 1], ring_to(way, n))
+
+    def gather_arrived(way, g, distance):
+        arrived(gather_slot(way, g, distance), ag_send.at[0], ag_recv.at[way, g, distance - 1], ring_to(way))
 
     def windows():
         for load in loads[2:4]:
@@ -207,8 +209,6 @@
     slices = size // 32
 
     def start_tables():
-        for d in range(J - 1):
-            arrived(info.at[(j + J - 1 - d) % J], info_send.at[0], info_recv.at[d], siblings[d])
         turn_cos, turn_sin = phases()
         for q in range(src_count):
             factors(q, turn_cos, turn_sin)
@@ -221,12 +221,26 @@
         for way in range(2):
             gather_send(way, g, 0)
 
-    def relay(g, h):
-        for way in range(2):
-            if h <= hops(way, g):
-                gather_arrived(way, g, h - 1)
-                if h < hops(way, g):
-                    gather_send(way, g, h)
+    def second(g):
+        up = long_way(g)
+        gather_arrived(up, g, 1)
+        gather_send(up, g, 1, 2)
+        gather_send(up, g, 1)
+        gather_arrived(1 - up, g, 1)
+        gather_send(1 - up, g, 1)
+
+    def third(g):
+        up = long_way(g)
+        gather_arrived(up, g, 3)
+        gather_send(up, g, 3)
+        gather_arrived(1 - up, g, 2)
+        gather_send(1 - up, g, 2)
+
+    def gathered(g):
+        up = long_way(g)
+        gather_arrived(up, g, 2)
+        gather_arrived(up, g, 4)
+        gather_arrived(1 - up, g, 3)
 
     def masked(values, g):
         mask = support[g * span : (g + 1) * span, :].astype(jnp.float32)
@@ -234,7 +248,7 @@
         return values * jnp.concatenate([mask] * (values.shape[0] // span), axis=0)
 
     def pupils(g):
-        relay(g, half)
+        gathered(g)
         summed = jnp.dot(mix[...], coeff[group(g), :], preferred_element_type=jnp.float32)
         pupil_out[group(g), :] = masked(summed, g).astype(jnp.bfloat16)
         for d, peer in enumerate(peers):
@@ -244,28 +258,47 @@
             )
         pupil_in[rows_of(me_r, g), :] = pupil_out[rows_of(me_r, g), :]
 
-    def build(step, first, last, parts, count):
-        lax.fori_loop(first * count // parts, last * count // parts, step, 0)
-
-    for g in range(groups):
-        own(g)
+    def on_core(core, what):
+        pl.when(j % 2 == core)(what)
+
+    def build(step, *parts):
+        (start0, stop0), (start1, stop1) = parts
+        first = jnp.where(j % 2 == 0, start0, start1)
+        lax.fori_loop(first, jnp.where(j % 2 == 0, stop0, stop1), step, 0)
+
+    def build_both(step, start, stop):
+        lax.fori_loop(start, stop, step, 0)
+
+    def own_blocks():
+        for g in range(groups):
+            own(g)
+
+    def second_step():
+        for g in range(groups):
+            second(g)
+
+    on_core(1, own_blocks)
     for d, device in enumerate(siblings):
         send(info.at[j], info.at[j], info_send.at[0], info_recv.at[d], device)
     windows()
-    cols = 0
-    for h in range(1, half):
-        for g in range(groups):
-            relay(g, h)
-            if (h, g) == (1, groups - 1):
-                start_tables()
-                loads[1].wait()
-            if h > 1:
-                build(build_col, cols, cols + 1, 2 * groups, slices)
-                cols += 1
-    build(build_lanes, 0, 1, 2, bands)
+    on_core(1, second_step)
+    for d in range(J - 1):
+        arrived(info.at[(j + J - 1 - d) % J], info_send.at[0], info_recv.at[d], siblings[d])
+    on_core(0, own_blocks)
+    start_tables()
+    loads[1].wait()
+    build(build_col, (0, slices // 2), (0, slices // 2))
+    on_core(0, second_step)
+    build(build_lanes, (0, bands // 2), (0, 0))
+    build(build_row, (0, slices // 4), (0, 0))
+    for g in range(groups):
+        third(g)
+        build_both(build_col, (groups + g) * slices // 8, (groups + g + 1) * slices // 8)
+    build(build_row, (slices // 4, slices // 2), (0, 0))
     for g in range(groups):
         pupils(g)
-    build(build_lanes, 1, 2, 2, bands)
+    build(build_lanes, (bands // 2, bands), (0, bands))
+    build(build_row, (slices // 2, slices), (0, slices // 4))
 
     def exchanged(landed, send_sem, recv_sem, g):
         blocks = landed.at[g * slab : g * slab + len(peers) * span, :]
@@ -314,12 +347,11 @@
 
         lax.fori_loop(0, bands, step, 0, unroll=True)
 
+    loads[6].wait()
     spectra(0)
-    build(build_row, 0, 1, 2, slices)
     spectra(1)
     images(0)
-    build(build_row, 1, 2, 2, slices)
-    loads[6].wait()
+    build(build_row, (0, 0), (slices // 4, slices))
     spectra(2)
     spectra(3)
     images(2)
@@ -339,13 +371,7 @@
             )
         returned[rows_of(me_r, g), :] = pulled[rows_of(me_r, g), :]
 
-    def target(way, g, t):
-        away = hops(way, g) - t
-        return (z + away) % ring if way == 0 else (z + ring - away) % ring
-
-    def scatter_slot(way, g, t, k):
-        if way == 1 and t == hops(way, g) - 1:
-            return part_in.at[g, ring * span : (ring + 1) * span, :]
+    def scatter_slot(g, k):
         return part_in.at[g, rows_of(k), :]
 
     def coded(values):
@@ -360,43 +386,37 @@
         scale = jnp.concatenate([jnp.exp2(power) * (1.0 / LEVELS)] * (2 * size // 128), axis=1)
         return slot[:, 0 : 2 * size].astype(jnp.int32).astype(jnp.float32) * scale
 
-    def scatter_send(way, g, t):
-        k = target(way, g, t)
+    def scatter_send(g, k, slot, arrival, device):
         levels, power = coded(part[rows_of(k, g), :])
         part_out[rows_of(k, g), 0 : 2 * size] = levels
         part_out[rows_of(k, g), 2 * size :] = power
-        send(
-            part_out.at[rows_of(k, g), :], scatter_slot(way, g, t, k),
-            rs_send.at[0], rs_recv.at[way, g, t], ring_to(way),
-        )
-
-    def scatter_arrived(way, g, t):
-        k = target(way, g, t + 1) if t + 1 < hops(way, g) else z
-        slot = scatter_slot(way, g, t, k)
-        arrived(slot, rs_send.at[0], rs_recv.at[way, g, t], ring_to(way))
-        return k
+        send(part_out.at[rows_of(k, g), :], scatter_slot(g, slot), rs_send.at[0], rs_recv.at[g, arrival], device)
+
+    def scatter_arrived(g, slot, arrival):
+        arrived(scatter_slot(g, slot), rs_send.at[0], rs_recv.at[g, arrival], right)
+        return decoded(scatter_slot(g, slot))
 
     def collect(g):
+        up = long_way(g)
         exchanged(returned, back_send, back_recv, g)
         part[group(g), :] = jnp.dot(mix_t[...], returned[group(g), :], preferred_element_type=jnp.float32)
-        for way in range(2):
-            scatter_send(way, g, 0)
-
-    def advance(g, t):
-        for way in range(2):
-            if t < hops(way, g):
-                k = scatter_arrived(way, g, t - 1)
-                part[rows_of(k, g), :] = part[rows_of(k, g), :] + decoded(part_in.at[g, rows_of(k), :])
-                scatter_send(way, g, t)
-
-    factor = 4.0 / (bands * total_slits)
+        scatter_send(g, ahead(up, 4), ahead(up, 4), 0, ring_to(up))
+        scatter_send(g, ahead(1 - up, 3), ahead(1 - up, 3), 1, ring_to(1 - up))
+        scatter_send(g, ahead(up, 2), ahead(up, 2), 2, ring_to(up))
+        scatter_send(g, ahead(1 - up, 1), ring, 3, ring_to(1 - up))
+
+    def combine(g):
+        up = long_way(g)
+        for way, n, arrival, slot in ((up, 3, 0, ring + 2), (1 - up, 2, 1, ring + 1), (up, 1, 2, None)):
+            k = ahead(way, n)
+            part[rows_of(k, g), :] = part[rows_of(k, g), :] + scatter_arrived(g, k, arrival)
+            scatter_send(g, k, k if slot is None else slot, arrival + 4, ring_to(way, n))
+
     leaving = []
 
     def finish(g):
-        for way in range(2):
-            scatter_arrived(way, g, hops(way, g) - 1)
-        total = part[rows_of(z, g), :] + decoded(part_in.at[g, rows_of(z), :])
-        total = (total + decoded(part_in.at[g, ring * span : (ring + 1) * span, :])) * factor
+        total = part[rows_of(z, g), :] + scatter_arrived(g, ring, 3)
+        total = total + scatter_arrived(g, ring + 2, 4) + scatter_arrived(g, ring + 1, 5) + scatter_arrived(g, z, 6)
         total = masked(total, g)
         for c in range(2):
             out[g, c] = total[:, c * size : (c + 1) * size]
@@ -406,14 +426,9 @@
 
     for g in range(groups):
         pull(g)
-    for slot in range(groups + half):
-        if slot < groups:
-            collect(slot)
-        for t in range(1, half):
-            if 0 <= slot - t < groups:
-                advance(slot - t, t)
-        if 0 <= slot - half < groups:
-            finish(slot - half)
+    for stage in (collect, combine, finish):
+        for g in range(groups):
+            stage(g)
 
     rounds = (ring - 1) * groups * span
     for moved, count, sem in (
@@ -445,8 +460,8 @@
     half = ring // 2
     peers = row_count - 1
     f32, bf16 = jnp.float32, jnp.bfloat16
-    return pl.pallas_call(
-        functools.partial(body, (ring, row_count, src_count, plane_count, size, total_slits)),
+    sums = pl.pallas_call(
+        functools.partial(body, (ring, row_count, src_count, plane_count, size)),
         out_shape=jax.ShapeDtypeStruct(direction.shape, jnp.float32),
         in_specs=[smem] * 4 + [hbm] * 7,
         out_specs=hbm,
@@ -481,7 +496,7 @@
             pltpu.VMEM((GROUPS * slab, 2 * size), bf16),
             pltpu.VMEM((GROUPS * ring * span, 2 * size), f32),
             pltpu.VMEM((GROUPS * ring * span, 2 * size + 128), jnp.int16),
-            pltpu.VMEM((GROUPS, (ring + 1) * span, 2 * size + 128), jnp.int16),
+            pltpu.VMEM((GROUPS, (ring + 3) * span, 2 * size + 128), jnp.int16),
             pltpu.VMEM((GROUPS, 2, span, size), f32),
             dma((7,)),
             dma((GROUPS,)),
@@ -494,12 +509,13 @@
             dma((1,)),
             dma((GROUPS,)),
             dma((1,)),
-            dma((2, GROUPS, half)),
+            dma((GROUPS, ring - 1)),
         ],
         compiler_params=pltpu.CompilerParams(
             collective_id=0, has_side_effects=True, vmem_limit_bytes=56 * 1024 * 1024
         ),
     )(slits, sources, focus, slit_focus, direction, support, obj_rows, obj_cols, weights, ker_t, ker_n)
+    return sums * (4.0 / (bands * total_slits))
 
 
 def solution(mesh):

time: 68.8 us -> 62 us (0.901)
  the two profiles are of different devices: /device:TPU:34 before, /device:TPU:6 now
where the time goes in v3:
time: 62 us; the launch traced here: 61.9 us
  Pallas kernels  60.2 us (97%)
  other arithmetic  1.68 us (3%)
    pallas_call x1, Pallas kernels, local(): pl.pallas_call(functools.partial(body, (ring, row_count, src_count, plane...  60.2 us
    mul x1, other arithmetic, local(): return sums * (4.0 / (bands * total_slits))  1.68 us

profile of v3, /device:TPU:6, one launch (start us, length us, event | category | flops | bytes accessed | tf_op | source)
XLA Modules:
  0.0 61.9 jit_solution(13350602732267282775)
XLA Ops:
  0.0 60.2 %shard_map.109 = f32[1,2,64,512]{3,2,1,0:T(8,128)} custom-call(s32[2]{0:T(128)} %slits.1, s32[4]{0:T(128)} %sources.1, f32[3]{0:T(128)} %focus.1, f32[2]{0:T(128)} %slit_focus.1, bf16[1,2,64,512]{3,2,1,0:T(8,128)(2,1)} %direction_hbm.1, s32[64,512]{1,0:T(8,128)} %support_hbm.1, f32[2,576]{1,0:T(2,128)} %obj_rows_hbm.1, f32[2,576]{1,0:T(2,128)} %obj_cols_hbm.1, ...), custom_call_target="tpu_custom_call" | custom-call | tf_op jit(solution)/shard_map/pallas_call | solution.py:463
  60.2 1.7 %broadcast_multiply_fusion = f32[1,2,64,512]{3,2,1,0:T(8,128)} fusion(f32[1,2,64,512]{3,2,1,0:T(8,128)} %shard_map.109), kind=kLoop, calls=%fused_computation | loop fusion | flops 65536 | bytes 524288 | tf_op jit(solution)/shard_map/mul | solution.py:518

commit v4 on v3

--- a/solution.py
+++ b/solution.py
@@ -37,7 +37,7 @@
 
 def body(sizes, slits, sources, focus, slit_focus, direction_hbm, support_hbm, obj_rows_hbm, obj_cols_hbm, weights_hbm,
          ker_t_hbm, ker_n_hbm, out_hbm,
-         direction, support, obj_rows, obj_cols, weights, ker_t, ker_n, info, coeff, mix, mix_t, pick, fac, fac_c, fac_t, fac_p,
+         direction, support, obj_rows, obj_cols, weights, ker_t, ker_n, info, coeff, mix, mix_t, raw, raw_t, raw_p, fac,
          col_t, row_t, col_n, row_n, pupil_out, pupil_in, spec, image, adj_re, adj_im, pulled, returned, part, part_out, part_in, out,
          load_sem, out_sem, info_send, info_recv, ag_send, ag_recv, out_send, out_recv, back_send, back_recv, rs_send, rs_recv):
     ring, row_count, src_count, plane_count, size = sizes
@@ -129,7 +129,7 @@
                 picked = shifted[0]
                 for v in range(1, SRC_SIDE):
                     picked = jnp.where(place == v, shifted[v], picked)
-                pick[axis, 8 * q : 8 * q + 2, :] = picked
+                raw[16 + 32 * axis + 8 * q : 18 + 32 * axis + 8 * q, :] = picked
 
     def phases():
         own_focus = info[me_r // 2, pl.ds((2 + me_r % 2) * span, 8), :]
@@ -141,22 +141,26 @@
         freq = lax.broadcasted_iota(jnp.int32, (8, size), 1)
         scaled = (2 * freq - size + 1).astype(jnp.float32) / size
         theta = math.pi * (plane + own_focus) * (scaled * scaled)
-        return jnp.cos(theta), jnp.sin(theta)
-
-    def factors(q, turn_cos, turn_sin):
-        for axis in range(2):
-            first, second = pick[axis, 8 * q : 8 * q + 1, :], pick[axis, 8 * q + 1 : 8 * q + 2, :]
+        raw[0:8, :] = jnp.cos(theta)
+        raw[8:16, :] = jnp.sin(theta)
+
+    def factors(axis, source):
+        turn_cos, turn_sin = source[0:8, :], source[8:16, :]
+        for q in range(src_count):
+            start = 16 + 32 * axis + 8 * q
+            first, second = source[start : start + 1, :], source[start + 1 : start + 2, :]
             base = 64 * axis + 8 * q
             fac[base : base + 8, :] = first * turn_cos - second * turn_sin
             fac[base + 32 : base + 40, :] = first * turn_sin + second * turn_cos
 
     def turn_factors():
-        fac_c[...] = fac[...].T
+        raw_t[...] = raw[...].T
         for g in range(groups):
             for r in range(row_count):
                 start = r * groups * span + g * span
-                fac_t[g * slab + r * span : g * slab + (r + 1) * span, :] = fac_c[start : start + span, :]
-        fac_p[...] = fac_t[...].T
+                raw_p[g * slab + r * span : g * slab + (r + 1) * span, :] = raw_t[start : start + span, :]
+        factors(0, raw_p[...].T)
+        factors(1, raw[...])
 
     def mixing():
         edge = row_count * span
@@ -179,7 +183,7 @@
     def build_lanes(band, carry):
         index = index_of(band)
         cf_re, cf_im = fac[pl.ds(64 + index, 1), :], fac[pl.ds(96 + index, 1), :]
-        rf_re, rf_im = fac_p[pl.ds(index, 1), :], fac_p[pl.ds(32 + index, 1), :]
+        rf_re, rf_im = fac[pl.ds(index, 1), :], fac[pl.ds(32 + index, 1), :]
         col_base, row_base = pl.multiple_of(band * M, M), pl.multiple_of(band * 2 * M, 2 * M)
         for m in range(0, M, 16):
             ker_re, ker_im = ker_t[0, 0, m : m + 16, :], ker_t[0, 1, m : m + 16, :]
@@ -190,28 +194,33 @@
             row_t[pl.ds(row_base + M + m, 16), :] = (rf_re * ker_im + rf_im * ker_re).astype(jnp.bfloat16)
         return carry
 
-    def build_sublanes(axis, held, offset, table):
+    def build_sublanes(axis, held, table):
         def step(i, carry):
             at = pl.ds(pl.multiple_of(i * 32, 32), 32)
-            ker_re, ker_im = ker_n[axis, 0, at, :], ker_n[axis, 1, at, :]
+            ker_re, ker_im = ker_n[1 - axis, 0, at, :], ker_n[1 - axis, 1, at, :]
             values = held[at, :]
-            for band in range(bands):
-                index = offset + index_of(band)
-                f_re, f_im = values[:, index : index + 1], values[:, 32 + index : 33 + index]
-                table[band, at, 0:M] = (f_re * ker_re - f_im * ker_im).astype(jnp.bfloat16)
-                table[band, at, M : 2 * M] = (f_re * ker_im + f_im * ker_re).astype(jnp.bfloat16)
+            turned = []
+            for p in range(plane_count):
+                turn_cos, turn_sin = values[:, p : p + 1], values[:, 8 + p : 9 + p]
+                turned.append((turn_cos * ker_re - turn_sin * ker_im, turn_cos * ker_im + turn_sin * ker_re))
+            for q in range(src_count):
+                start = 16 + 32 * axis + 8 * q
+                first = jnp.broadcast_to(values[:, start : start + 1], (32, M))
+                second = jnp.broadcast_to(values[:, start + 1 : start + 2], (32, M))
+                for p, (real, imag) in enumerate(turned):
+                    band = q * plane_count + p
+                    table[band, at, 0:M] = (first * real - second * imag).astype(jnp.bfloat16)
+                    table[band, at, M : 2 * M] = (first * imag + second * real).astype(jnp.bfloat16)
             return carry
 
         return step
 
-    build_col = build_sublanes(0, fac_c, 64, col_n)
-    build_row = build_sublanes(1, fac_t, 0, row_n)
+    build_col = build_sublanes(1, raw_t, col_n)
+    build_row = build_sublanes(0, raw_p, row_n)
     slices = size // 32
 
     def start_tables():
-        turn_cos, turn_sin = phases()
-        for q in range(src_count):
-            factors(q, turn_cos, turn_sin)
+        phases()
         turn_factors()
         mixing()
         for load in loads[4:6]:
@@ -266,9 +275,6 @@
         first = jnp.where(j % 2 == 0, start0, start1)
         lax.fori_loop(first, jnp.where(j % 2 == 0, stop0, stop1), step, 0)
 
-    def build_both(step, start, stop):
-        lax.fori_loop(start, stop, step, 0)
-
     def own_blocks():
         for g in range(groups):
             own(g)
@@ -281,24 +287,25 @@
     for d, device in enumerate(siblings):
         send(info.at[j], info.at[j], info_send.at[0], info_recv.at[d], device)
     windows()
+    on_core(0, own_blocks)
     on_core(1, second_step)
     for d in range(J - 1):
         arrived(info.at[(j + J - 1 - d) % J], info_send.at[0], info_recv.at[d], siblings[d])
-    on_core(0, own_blocks)
     start_tables()
     loads[1].wait()
-    build(build_col, (0, slices // 2), (0, slices // 2))
     on_core(0, second_step)
     build(build_lanes, (0, bands // 2), (0, 0))
-    build(build_row, (0, slices // 4), (0, 0))
+    build(build_row, (0, slices // 2), (0, 0))
+    build(build_col, (0, slices // 2), (0, slices // 2))
     for g in range(groups):
         third(g)
-        build_both(build_col, (groups + g) * slices // 8, (groups + g + 1) * slices // 8)
-    build(build_row, (slices // 4, slices // 2), (0, 0))
+        build(build_row, (0, 0), (g * slices // 8, (g + 1) * slices // 8))
+    build(build_col, (slices // 2, slices), (slices // 2, 5 * slices // 8))
     for g in range(groups):
         pupils(g)
+    build(build_col, (0, 0), (5 * slices // 8, slices))
     build(build_lanes, (bands // 2, bands), (0, bands))
-    build(build_row, (slices // 2, slices), (0, slices // 4))
+    build(build_row, (slices // 2, slices), (0, 0))
 
     def exchanged(landed, send_sem, recv_sem, g):
         blocks = landed.at[g * slab : g * slab + len(peers) * span, :]
@@ -351,7 +358,7 @@
     spectra(0)
     spectra(1)
     images(0)
-    build(build_row, (0, 0), (slices // 4, slices))
+    build(build_row, (0, 0), (slices // 2, slices))
     spectra(2)
     spectra(3)
     images(2)
@@ -396,39 +403,90 @@
         arrived(scatter_slot(g, slot), rs_send.at[0], rs_recv.at[g, arrival], right)
         return decoded(scatter_slot(g, slot))
 
+    def take_in(g, k, slot, arrival):
+        part[rows_of(k, g), :] = part[rows_of(k, g), :] + scatter_arrived(g, slot, arrival)
+
     def collect(g):
         up = long_way(g)
         exchanged(returned, back_send, back_recv, g)
         part[group(g), :] = jnp.dot(mix_t[...], returned[group(g), :], preferred_element_type=jnp.float32)
         scatter_send(g, ahead(up, 4), ahead(up, 4), 0, ring_to(up))
         scatter_send(g, ahead(1 - up, 3), ahead(1 - up, 3), 1, ring_to(1 - up))
-        scatter_send(g, ahead(up, 2), ahead(up, 2), 2, ring_to(up))
-        scatter_send(g, ahead(1 - up, 1), ring, 3, ring_to(1 - up))
-
-    def combine(g):
+
+        def more():
+            scatter_send(g, ahead(up, 2), ahead(up, 2), 2, ring_to(up))
+            if g >= groups // 2:
+                scatter_send(g, ahead(1 - up, 1), ring, 3, ring_to(1 - up))
+
+        on_core(0, more)
+
+    def pass_on(g, way, n, arrival, slot, next_arrival):
+        k = ahead(way, n)
+        take_in(g, k, k, arrival)
+        scatter_send(g, k, k if slot is None else slot, next_arrival, ring_to(way))
+
+    def combine_two(g):
         up = long_way(g)
         for way, n, arrival, slot in ((up, 3, 0, ring + 2), (1 - up, 2, 1, ring + 1), (up, 1, 2, None)):
             k = ahead(way, n)
-            part[rows_of(k, g), :] = part[rows_of(k, g), :] + scatter_arrived(g, k, arrival)
+            take_in(g, k, k, arrival)
             scatter_send(g, k, k if slot is None else slot, arrival + 4, ring_to(way, n))
 
-    leaving = []
-
-    def finish(g):
-        total = part[rows_of(z, g), :] + scatter_arrived(g, ring, 3)
-        total = total + scatter_arrived(g, ring + 2, 4) + scatter_arrived(g, ring + 1, 5) + scatter_arrived(g, z, 6)
+    def combine_three(g):
+        up = long_way(g)
+        far, near = ahead(up, 3), ahead(1 - up, 2)
+        take_in(g, far, far, 0)
+        scatter_send(g, far, ring + 2, 4, ring_to(up, 2))
+        take_in(g, near, near, 1)
+        scatter_send(g, near, near, 5, ring_to(1 - up))
+
+    def deliver_three(g):
+        up = long_way(g)
+        first, other = ahead(up, 1), ahead(1 - up, 1)
+        take_in(g, other, other, 5)
+        scatter_send(g, other, ring, 3, ring_to(1 - up))
+        take_in(g, first, first, 2)
+        take_in(g, first, ring + 2, 4)
+        scatter_send(g, first, first, 6, ring_to(up))
+
+    def leave(g):
+        return pltpu.make_async_copy(out.at[g], out_hbm.at[0, :, g * span : (g + 1) * span, :], out_sem.at[g])
+
+    def finish(g, *arrivals):
+        total = part[rows_of(z, g), :] + scatter_arrived(g, z, 6)
+        for slot, arrival in arrivals:
+            total = total + scatter_arrived(g, slot, arrival)
         total = masked(total, g)
         for c in range(2):
             out[g, c] = total[:, c * size : (c + 1) * size]
-        leave = pltpu.make_async_copy(out.at[g], out_hbm.at[0, :, g * span : (g + 1) * span, :], out_sem.at[g])
-        leave.start()
-        leaving.append(leave)
+        leave(g).start()
+
+    def with_jumps():
+        for g in range(groups):
+            (combine_three if g < groups // 2 else combine_two)(g)
+        for g in range(groups // 2):
+            deliver_three(g)
+        for g in range(groups):
+            finish(g, *[(ring, 3), (ring + 2, 4), (ring + 1, 5)][: 1 if g < groups // 2 else 3])
+
+    def place_to_place():
+        for g in range(groups):
+            pass_on(g, long_way(g), 3, 0, None, 2)
+            pass_on(g, 1 - long_way(g), 2, 1, None, 4)
+        for g in range(groups):
+            pass_on(g, long_way(g), 2, 2, None, 5)
+            pass_on(g, 1 - long_way(g), 1, 4, ring, 3)
+        for g in range(groups):
+            pass_on(g, long_way(g), 1, 5, None, 6)
+        for g in range(groups):
+            finish(g, (ring, 3))
 
     for g in range(groups):
         pull(g)
-    for stage in (collect, combine, finish):
-        for g in range(groups):
-            stage(g)
+    for g in range(groups):
+        collect(g)
+    on_core(0, with_jumps)
+    on_core(1, place_to_place)
 
     rounds = (ring - 1) * groups * span
     for moved, count, sem in (
@@ -439,8 +497,8 @@
         pltpu.make_async_remote_copy(
             src_ref=all_sent, dst_ref=all_sent, send_sem=sem.at[0], recv_sem=sem.at[0], device_id=right, device_id_type=MESH
         ).wait_send()
-    for leave in leaving:
-        leave.wait()
+    for g in range(groups):
+        leave(g).wait()
 
 
 def local(direction, slits, sources, support, focus, slit_focus, obj_rows, obj_cols, weights):
@@ -477,7 +535,6 @@
             pltpu.VMEM((GROUPS * ring * span, 2 * size), bf16),
             pltpu.VMEM((slab, ring * span), bf16),
             pltpu.VMEM((ring * span, slab), bf16),
-            pltpu.VMEM((2, 8 * src_count, size), f32),
             pltpu.VMEM((128, size), f32),
             pltpu.VMEM((size, 128), f32),
             pltpu.VMEM((size, 128), f32),

time: 62 us -> 59.4 us (0.958)
  Pallas kernels: 60.2 us -> 57.3 us
    pallas_call x1, Pallas kernels: 60.2 us -> 57.3 us  [local(): pl.pallas_call(functools.partial(body, (ring, row_count, src_count, plane...]
where the time goes in v4:
time: 59.4 us; the launch traced here: 59 us
  Pallas kernels  57.3 us (96%)
  other arithmetic  1.68 us (3%)
    pallas_call x1, Pallas kernels, local(): pl.pallas_call(functools.partial(body, (ring, row_count, src_count, plane...  57.3 us
    mul x1, other arithmetic, local(): return sums * (4.0 / (bands * total_slits))  1.68 us

profile of v4, /device:TPU:6, one launch (start us, length us, event | category | flops | bytes accessed | tf_op | source)
XLA Modules:
  0.0 59.0 jit_solution(5702303335889345699)
XLA Ops:
  0.0 57.3 %shard_map.109 = f32[1,2,64,512]{3,2,1,0:T(8,128)} custom-call(s32[2]{0:T(128)} %slits.1, s32[4]{0:T(128)} %sources.1, f32[3]{0:T(128)} %focus.1, f32[2]{0:T(128)} %slit_focus.1, bf16[1,2,64,512]{3,2,1,0:T(8,128)(2,1)} %direction_hbm.1, s32[64,512]{1,0:T(8,128)} %support_hbm.1, f32[2,576]{1,0:T(2,128)} %obj_rows_hbm.1, f32[2,576]{1,0:T(2,128)} %obj_cols_hbm.1, ...), custom_call_target="tpu_custom_call" | custom-call | tf_op jit(solution)/shard_map/pallas_call | solution.py:521
  57.3 1.7 %broadcast_multiply_fusion = f32[1,2,64,512]{3,2,1,0:T(8,128)} fusion(f32[1,2,64,512]{3,2,1,0:T(8,128)} %shard_map.109), kind=kLoop, calls=%fused_computation | loop fusion | flops 65536 | bytes 524288 | tf_op jit(solution)/shard_map/mul | solution.py:575

commit v5 on v4

--- a/solution.py
+++ b/solution.py
@@ -59,7 +59,8 @@
 
     right = ring_to(0)
     siblings = [(z * J + (j + d) % J, me_r) for d in range(1, J)]
-    steps = [(dy, dx) for dy in (2, 1, 3, 0) for dx in (1, 0) if dy < y_count and (dy, dx) != (0, 0)]
+    steps = [(2, 1), (1, 0), (3, 1), (2, 0), (1, 1), (3, 0), (0, 1)]
+    steps = [(dy, dx) for dy, dx in steps if dy < y_count]
     peers = [((y + dy) % y_count) * 2 + (x + dx) % 2 for dy, dx in steps]
 
     barrier = pltpu.get_barrier_semaphore()

time: 59.4 us -> 60.6 us (1.020)
  Pallas kernels: 57.3 us -> 58.1 us
    pallas_call x1, Pallas kernels: 57.3 us -> 58.1 us  [local(): pl.pallas_call(functools.partial(body, (ring, row_count, src_count, plane...]
where the time goes in v5:
time: 60.6 us; the launch traced here: 59.8 us
  Pallas kernels  58.1 us (96%)
  other arithmetic  1.68 us (3%)
    pallas_call x1, Pallas kernels, local(): pl.pallas_call(functools.partial(body, (ring, row_count, src_count, plane...  58.1 us
    mul x1, other arithmetic, local(): return sums * (4.0 / (bands * total_slits))  1.68 us

profile of v5, /device:TPU:6, one launch (start us, length us, event | category | flops | bytes accessed | tf_op | source)
XLA Modules:
  0.0 59.8 jit_solution(12603845164499716060)
XLA Ops:
  0.0 58.1 %shard_map.109 = f32[1,2,64,512]{3,2,1,0:T(8,128)} custom-call(s32[2]{0:T(128)} %slits.1, s32[4]{0:T(128)} %sources.1, f32[3]{0:T(128)} %focus.1, f32[2]{0:T(128)} %slit_focus.1, bf16[1,2,64,512]{3,2,1,0:T(8,128)(2,1)} %direction_hbm.1, s32[64,512]{1,0:T(8,128)} %support_hbm.1, f32[2,576]{1,0:T(2,128)} %obj_rows_hbm.1, f32[2,576]{1,0:T(2,128)} %obj_cols_hbm.1, ...), custom_call_target="tpu_custom_call" | custom-call | tf_op jit(solution)/shard_map/pallas_call | solution.py:522
  58.1 1.7 %broadcast_multiply_fusion = f32[1,2,64,512]{3,2,1,0:T(8,128)} fusion(f32[1,2,64,512]{3,2,1,0:T(8,128)} %shard_map.109), kind=kLoop, calls=%fused_computation | loop fusion | flops 65536 | bytes 524288 | tf_op jit(solution)/shard_map/mul | solution.py:576
